TPU v7x, 128 devices: a whole 4x4x4 slice. The times are simulated.
128 devices in a mesh: tensor: 8 (over x_lo, y), ulysses: 16 (over z, x_hi, core).
Axes of the slice: x: 4 (x_hi: 2, x_lo: 2; x = x_hi * 2 + x_lo), y: 4, z: 4, core: 2. Of those that a mesh axis runs over, the one named last changes fastest.
Arguments:
- tokens: bfloat16 [1024, 16384], P('ulysses'), may hold values from -6 to 6
- q_weight: bfloat16 [16384, 16384], P('ulysses', 'tensor'), may hold values from -0.046875 to 0.046875
- k_weight: bfloat16 [16384, 1024], P('ulysses', 'tensor'), may hold values from -0.046875 to 0.046875
- v_weight: bfloat16 [16384, 1024], P('ulysses', 'tensor'), may hold values from -0.046875 to 0.046875
- cache_keys: bfloat16 [16384, 1024], P('ulysses', 'tensor'), may hold values from -160 to 160
- cache_values: bfloat16 [16384, 1024], P('ulysses', 'tensor'), may hold values from -6 to 6
- cache_len: int32 [1], replicated, may hold values from 8192 to 16384
- span_start: int32 [1], replicated, may hold values from 16384 to 32767
Outputs:
- attended: bfloat16 [1024, 16384], P(('tensor', 'ulysses'))
All inputs are finite; a program needn't handle non-finite values.
Results may differ from a plain program's by a relative error of at most 0.014.
The roundings to bfloat16 on the way count: a program that leaves them out, or rounds other values in their place, can miss the bound.
Values may be sent and summed in bfloat16 or wider, within the bound.
No kernel may reach another device: no remote copies, remote signals or barrier semaphores. Data moves between devices by JAX's collectives and lax.ppermute only.
A program may use at most 128 MiB of HBM per device.

v0:
```python
import math

import jax
import jax.numpy as jnp
from jax import lax
from jax.sharding import PartitionSpec as P

HD = 128


def angle_table(positions, head_size):
    steps = jnp.arange(head_size // 2).astype(jnp.float32)
    freq = jnp.exp(-(2.0 * steps / head_size) * math.log(500000.0))
    return positions.astype(jnp.float32)[:, None] * freq[None, :]


def rotate(values, cos_t, sin_t, axis):
    first, second = jnp.split(values, 2, axis=axis)
    return jnp.concatenate(
        [first * cos_t - second * sin_t, second * cos_t + first * sin_t], axis=axis
    )


def on_device(
    tokens, q_weight, k_weight, v_weight, cache_keys, cache_values, cache_len, span_start
):
    n_tensor = lax.axis_size("tensor")
    n_ulysses = lax.axis_size("ulysses")
    scale = 1.0 / math.sqrt(HD)
    spread = lax.all_to_all(tokens, "ulysses", split_axis=1, concat_axis=0, tiled=True)
    span = spread.shape[0]
    weight_rows = q_weight.shape[0]
    groups = k_weight.shape[1] // HD
    q_cols = q_weight.shape[1]
    group_heads = q_cols // (groups * HD)
    local_heads = group_heads // n_ulysses
    width = groups * HD
    angles = angle_table(span_start[0] + jnp.arange(span, dtype=jnp.int32), HD)
    cos_t = jnp.cos(angles)
    sin_t = jnp.sin(angles)
    both_weights = jnp.concatenate([k_weight, v_weight], axis=1)
    weight_four = q_weight.reshape(weight_rows, groups, group_heads, HD)
    term = lax.dot_general(
        weight_four, spread, (((0,), (1,)), ((), ())), preferred_element_type=jnp.float32
    )
    q_mine = lax.psum_scatter(
        jnp.transpose(term, (1, 0, 2, 3)).reshape(
            q_cols // n_ulysses * lax.axis_size("ulysses"), span
        ),
        "ulysses",
        scatter_dimension=0,
        tiled=True,
    )
    q_rot = rotate(q_mine.reshape(local_heads, groups, HD, span), cos_t.T, sin_t.T, 2).astype(
        jnp.bfloat16
    )
    kv_part = jnp.dot(spread, both_weights, preferred_element_type=jnp.float32)
    kv_all = lax.psum(kv_part.astype(jnp.bfloat16), "ulysses").astype(jnp.float32)
    k_rot = rotate(
        kv_all[:, :width].reshape(span, groups, HD), cos_t[:, None, :], sin_t[:, None, :], 2
    ).astype(jnp.bfloat16)
    v_rows = kv_all[:, width:].astype(jnp.bfloat16).reshape(span, groups, HD)
    index = jnp.arange(span, dtype=jnp.int32)
    block_seen = (index[:, None] <= index[None, :])[None, None, :, :]
    scores = jnp.einsum("jgd,hgdc->hgjc", k_rot, q_rot, preferred_element_type=jnp.float32) * scale
    top = jnp.max(jnp.where(block_seen, scores, -1e30), axis=2)
    weights = jnp.where(block_seen, jnp.exp(scores - top[:, :, None, :]), 0.0)
    total = jnp.sum(weights, axis=2)
    accum = jnp.einsum(
        "jgd,hgjc->hgdc", v_rows, weights.astype(jnp.bfloat16), preferred_element_type=jnp.float32
    )
    keys_piece = lax.all_gather(cache_keys, "ulysses", axis=0, tiled=True)
    values_piece = lax.all_gather(cache_values, "ulysses", axis=0, tiled=True)
    count = keys_piece.shape[0]
    block = math.gcd(count, 1024)

    def one_block(step, state):
        top_now, total_now, accum_now = state
        key_block = lax.dynamic_slice_in_dim(keys_piece, step * block, block, 0).reshape(
            block, groups, HD
        )
        value_block = lax.dynamic_slice_in_dim(values_piece, step * block, block, 0).reshape(
            block, groups, HD
        )
        block_scores = (
            jnp.einsum("jgd,hgdc->hgjc", key_block, q_rot, preferred_element_type=jnp.float32)
            * scale
        )
        live = step * block + jnp.arange(block, dtype=jnp.int32) < cache_len[0]
        live_four = live[None, None, :, None]
        block_top = jnp.max(jnp.where(live_four, block_scores, -1e30), axis=2)
        new_top = jnp.maximum(top_now, block_top)
        block_weights = jnp.where(live_four, jnp.exp(block_scores - new_top[:, :, None, :]), 0.0)
        factor = jnp.exp(top_now - new_top)
        new_total = total_now * factor + jnp.sum(block_weights, axis=2)
        added = jnp.einsum(
            "jgd,hgjc->hgdc",
            value_block,
            block_weights.astype(jnp.bfloat16),
            preferred_element_type=jnp.float32,
        )
        return (new_top, new_total, accum_now * factor[:, :, None, :] + added)

    top, total, accum = lax.fori_loop(0, count // block, one_block, (top, total, accum))
    mixed = (accum / total[:, :, None, :]).astype(jnp.bfloat16)
    arranged = jnp.transpose(mixed, (3, 1, 0, 2)).reshape(span, 1, 1, groups, local_heads, HD)
    out_rows = span // (n_tensor * n_ulysses)
    moved = lax.all_to_all(arranged, ("tensor", "ulysses"), split_axis=0, concat_axis=1, tiled=True)
    moved = moved.reshape(out_rows, n_tensor, n_ulysses, groups, local_heads, HD)
    return jnp.transpose(moved, (0, 1, 3, 2, 4, 5)).reshape(
        out_rows, n_tensor * groups * n_ulysses * local_heads * HD
    )


def solution(mesh):
    placed = (
        P("ulysses", None),
        P("ulysses", "tensor"),
        P("ulysses", "tensor"),
        P("ulysses", "tensor"),
        P("ulysses", "tensor"),
        P("ulysses", "tensor"),
        P(),
        P(),
    )
    return jax.shard_map(
        on_device,
        mesh=mesh,
        in_specs=placed,
        out_specs=P(("tensor", "ulysses"), None),
        check_vma=False,
    )
```

profile of v0, /device:TPU:1, one launch (start us, length us, event | category | flops | bytes accessed | tf_op | source)
XLA Modules:
  0.0 522.5 jit_solution(4345794659753096831)
XLA Ops:
  6.5 3.2 copy.23
  9.7 9.3 %all-to-all-start = ((bf16[64,16,1024]{2,0,1:T(8,128)(2,1)}), bf16[64,16,1024]{2,0,1:T(8,128)(2,1)S(1)}, u32[]{:S(2)}, u32[]{:S(2)}) async-start(bf16[64,16,1024]{2,0,1:T(8,128)(2,1)} %bitcast.122), calls=%async_computation | async-start | bytes 4194304 | tf_op jit(solution)/shard_map/all_to_all | solution.py:30
  19.1 5.6 %copy.15 = bf16[128,8,16,128]{3,2,1,0:T(8,128)(2,1)} copy(bf16[128,8,16,128]{3,1,2,0:T(8,128)(2,1)} %bitcast.147) | data formatting | bytes 8388608
  24.7 22.8 %all-to-all-done = bf16[64,16,1024]{2,0,1:T(8,128)(2,1)S(1)} async-done(((bf16[64,16,1024]{2,0,1:T(8,128)(2,1)}), bf16[64,16,1024]{2,0,1:T(8,128)(2,1)S(1)}, u32[]{:S(2)}, u32[]{:S(2)}) %all-to-all-start) | async-done | bytes 2097184 | tf_op jit(solution)/shard_map/all_to_all | solution.py:30
  49.1 9.3 %fusion.23 = f32[2048,1024]{1,0:T(8,128)} fusion(bf16[1024,1024]{1,0:T(8,128)(2,1)S(1)} %bitcast.150, bf16[128,8,16,128]{3,2,1,0:T(8,128)(2,1)} %copy.15), kind=kOutput, calls=%fused_computation.23 | convolution fusion | flops 4294967296 | bytes 14680064 | tf_op jit(solution)/shard_map/dot_general | solution.py:43
  60.4 125.4 %all-reduce.2.cloned.1.call-done = bf16[1024,256]{0,1:T(8,128)(2,1)} async-done(((bf16[1024,256]{0,1:T(8,128)(2,1)}), bf16[1024,256]{0,1:T(8,128)(2,1)}) %all-reduce.2.cloned.1.call-update) | async-done | bytes 524304 | tf_op jit(solution)/shard_map/psum | solution.py:58
  187.9 105.1 %reduce-scatter.2.cloned.1.call-done = f32[128,1024]{1,0:T(8,128)} async-done(((f32[2048,1024]{1,0:T(8,128)}), f32[128,1024]{1,0:T(8,128)}) %reduce-scatter.2.cloned.1.call-update) | async-done | bytes 524304 | tf_op jit(solution)/shard_map/reduce_scatter | solution.py:46
  293.0 2.1 fusion.54
  297.7 53.8 %all-gather.3.cloned.1.call-done = bf16[16384,128]{1,0:T(8,128)(2,1)} async-done(((bf16[1024,128]{1,0:T(8,128)(2,1)}), bf16[16384,128]{1,0:T(8,128)(2,1)}) %all-gather.3.cloned.1.call-update) | async-done | bytes 4194320 | tf_op jit(solution)/shard_map/all_gather | solution.py:72
  351.5 55.9 %all-gather.5.cloned.1.call-done = bf16[16384,128]{1,0:T(8,128)(2,1)} async-done(((bf16[1024,128]{1,0:T(8,128)(2,1)}), bf16[16384,128]{1,0:T(8,128)(2,1)}) %all-gather.5.cloned.1.call-update) | async-done | bytes 4194320 | tf_op jit(solution)/shard_map/all_gather | solution.py:73
  407.4 89.3 %while.17 = (s32[]{:T(128)}, f32[1,1,1024]{2,1,0:T(1,128)S(1)}, f32[1,1,1024]{2,1,0:T(1,128)S(1)}, f32[1,1,128,1024]{2,3,0,1:T(8,128)S(1)}, s32[1]{0:T(128)}, /*...) while((s32[]{:T(128)}, f32[1,1,1024]{2,1,0:T(1,128)S(1)}, ...), condition=%wide.region_7.8_spmd, body=%wide.region_4.7_spmd.sunk | while | flops 548671488 | bytes 14487731 | solution.py:104
  408.0 1.7 fusion.82
  410.6 2.3 fusion.84
  416.2 2.3 fusion.84
  419.2 1.7 fusion.82
  421.8 2.3 fusion.84
  424.8 1.7 fusion.82
  427.4 2.3 fusion.84
  433.0 2.3 fusion.84
  438.6 2.3 fusion.84
  444.1 2.3 fusion.84
  449.7 2.3 fusion.84
  455.3 2.3 fusion.84
  460.9 2.3 fusion.84
  466.5 2.3 fusion.84
  472.1 2.3 fusion.84
  477.6 2.3 fusion.84
  483.2 2.3 fusion.84
  486.2 1.7 fusion.82
  488.8 2.3 fusion.84
  494.4 2.3 fusion.84
  498.4 16.6 %all_to_all.34 = bf16[128,2,512]{2,1,0:T(2,128)(2,1)S(1)} all-to-all(bf16[128,2,512]{2,1,0:T(2,128)(2,1)S(1)} %reshape.350), channel_id=1, replica_groups=mesh['tensor'=8,'ulysses'=16] {'tensor','ulysses'}, dimensions={0} | all-to-all | bytes 524288 | tf_op jit(solution)/shard_map/all_to_all | solution.py:108
  (121 shorter events, 55.1 us)
Async XLA Ops:
  9.7 37.8 %all-to-all-start = ((bf16[64,16,1024]{2,0,1:T(8,128)(2,1)}), bf16[64,16,1024]{2,0,1:T(8,128)(2,1)S(1)}, u32[]{:S(2)}, u32[]{:S(2)}) async-start(bf16[64,16,1024]{2,0,1:T(8,128)(2,1)} %bitcast.122), calls=%async_computation | async-start | bytes 4194304 | tf_op jit(solution)/shard_map/all_to_all | solution.py:30
  19.0 166.8 %all-reduce.2.cloned.1.call-start = ((), (), s32[]{:S(2)}) async-start(), calls=%async_computation.4 | async-start | bytes 1048576 | tf_op jit(solution)/shard_map/psum | solution.py:58
  19.0 28.4 %copy-start.1 = (bf16[1024,128]{1,0:T(8,128)(2,1)S(1)}, bf16[1024,128]{1,0:T(8,128)(2,1)}, u32[]{:S(2)}) copy-start(bf16[1024,128]{1,0:T(8,128)(2,1)} %param.13) | copy-start | bytes 786436
  19.1 28.4 %copy-start.2 = (bf16[1024,128]{1,0:T(8,128)(2,1)S(1)}, bf16[1024,128]{1,0:T(8,128)(2,1)}, u32[]{:S(2)}) copy-start(bf16[1024,128]{1,0:T(8,128)(2,1)} %param.12) | copy-start | bytes 786436
  49.1 244.0 %reduce-scatter.2.cloned.1.call-start = ((), (), s32[]{:S(2)}) async-start(), calls=%async_computation.3 | async-start | bytes 8912896 | tf_op jit(solution)/shard_map/reduce_scatter | solution.py:46
  58.4 293.1 %all-gather.3.cloned.1.call-start = ((), (), s32[]{:S(2)}) async-start(), calls=%async_computation.5 | async-start | bytes 4456448 | tf_op jit(solution)/shard_map/all_gather | solution.py:72
  59.1 348.2 %all-gather.5.cloned.1.call-start = ((), (), s32[]{:S(2)}) async-start(), calls=%async_computation.6 | async-start | bytes 4456448 | tf_op jit(solution)/shard_map/all_gather | solution.py:73
  295.9 1.0 copy-start
Sparse Core Ops, SparseCore 0:
  49.2 136.5 all-reduce.1
  190.6 102.3 reduce-scatter.1
  295.8 55.6 all-gather.2
  354.1 53.1 all-gather.4
where the time goes:
time: 524 us; the launch traced here: 522 us
  waiting for transfers between devices  364 us (69%)
  matrix products  75.9 us (14%)
  other arithmetic  30.4 us (6%)
  blocking collectives  16.6 us (3%)
  between operations  13.9 us (3%)
  local copies, waits for them, and re-layouts  11 us (2%)
  starting transfers between devices  9.45 us (2%)
    psum x1, waiting for transfers between devices, on_device(): lax.psum(kv_part.astype(jnp.bfloat16), 'ulysses').astype(jnp.float32)  125 us
    reduce_scatter x1, waiting for transfers between devices, on_device(): lax.psum_scatter(jnp.transpose(term, (1, 0, 2, 3)).reshape(q_cols // n_ul...  105 us
    all_gather x1, waiting for transfers between devices, on_device(): values_piece = lax.all_gather(cache_values, 'ulysses', axis=0, tiled=True)  55.9 us
    all_gather x1, waiting for transfers between devices, on_device(): keys_piece = lax.all_gather(cache_keys, 'ulysses', axis=0, tiled=True)  53.8 us
    dot_general x16, matrix products, one_block(): jnp.einsum('jgd,hgjc->hgdc', value_block, block_weights.astype(jnp.bfloat...  36.6 us
    dot_general x16, matrix products, one_block(): jnp.einsum('jgd,hgdc->hgjc', key_block, q_rot, preferred_element_type=jnp...  27 us
    all_to_all x1, waiting for transfers between devices, on_device(): lax.all_to_all(tokens, 'ulysses', split_axis=1, concat_axis=0, tiled=True)  22.8 us
    all_to_all x1, blocking collectives, on_device(): lax.all_to_all(arranged, ('tensor', 'ulysses'), split_axis=0, concat_axis...  16.6 us
  transfers between devices with their start and end apart: 5, of which 5 were waited for; matrix products, arithmetic and copies ran while one was open for 4% of the time, Pallas kernels for 0%

commit v1 on v0

v1 whole, which is shorter than its diff:
```python
import functools
import math

import jax
import jax.numpy as jnp
from jax import lax
from jax.experimental import pallas as pl
from jax.experimental.pallas import tpu as pltpu
from jax.sharding import PartitionSpec as P

HD = 128
NZ, NX, NC = 4, 2, 2
CHIPS = NZ * NX
SPAN = 1024
ROWS = 1024
SCALE2 = math.log2(math.e) / math.sqrt(HD)
BOOST = 64.0
NEG = -1e30


def angle_table(positions, head_size):
    steps = jnp.arange(head_size // 2).astype(jnp.float32)
    freq = jnp.exp(-(2.0 * steps / head_size) * math.log(500000.0))
    return positions.astype(jnp.float32)[:, None] * freq[None, :]


def rotate(values, cos_t, sin_t, axis):
    first, second = jnp.split(values, 2, axis=axis)
    return jnp.concatenate(
        [first * cos_t - second * sin_t, second * cos_t + first * sin_t], axis=axis
    )


def unit(z, x, c):
    return (z % NZ) * NX * NC + (x % NX) * NC + c % NC


def hop(values, dz=0, dx=0, dc=0):
    pairs = [
        (unit(z, x, c), unit(z + dz, x + dx, c + dc))
        for z in range(NZ)
        for x in range(NX)
        for c in range(NC)
    ]
    return lax.ppermute(values, "ulysses", pairs)


SAME_CORE = [[NC * p + c for p in range(CHIPS)] for c in range(NC)]


def chunk_cols(block, first, count):
    parts = [block[pl.ds(first + HD * i, HD), :] for i in range(count)]
    return jnp.concatenate(parts, axis=1)


def attention_kernel(n_blocks, meta, q_ref, new_ref, *rest):
    blocks = rest[:n_blocks]
    o_ref, held, sems = rest[n_blocks:]
    core = meta[1]
    live = meta[0]
    span = q_ref.shape[0]
    half = span // 2
    piece = half // CHIPS
    copies = []
    for i, block in enumerate(blocks):
        slot = meta[2 + i]
        copies.append(pltpu.make_async_copy(block, held.at[slot], sems.at[slot]))
    for copy in copies:
        copy.start()

    col = lax.broadcasted_iota(jnp.int32, (1, span), 1)
    own = jnp.where(col < half, core, 1 - core)
    inside = col % half
    query = (inside // piece) * (2 * piece) + own * piece + inside % piece
    q = q_ref[...]

    def scores_of(keys):
        return lax.dot_general(
            keys, q, (((1,), (1,)), ((), ())), preferred_element_type=jnp.float32
        )

    def add_values(cols, p):
        return lax.dot_general(
            cols, p.astype(jnp.bfloat16), (((1,), (0,)), ((), ())),
            preferred_element_type=jnp.float32,
        )

    def fold(p):
        return jnp.sum(p.reshape(p.shape[0] // 8, 8, p.shape[1]), axis=0)

    def wait_for(slot):
        pltpu.make_async_copy(blocks[0], held.at[slot], sems.at[slot]).wait()

    def direct(keys, cols, state, seen=None):
        acc, total = state
        p = jnp.exp2(scores_of(keys) * SCALE2)
        if seen is not None:
            p = jnp.where(seen(p.shape), p, 0.0)
        return acc + add_values(cols, p), total + fold(p)

    def causal(shape):
        return lax.broadcasted_iota(jnp.int32, shape, 0) <= query

    state = (jnp.zeros((HD, span), jnp.float32), jnp.zeros((8, span), jnp.float32))
    state = direct(new_ref[:ROWS, :], chunk_cols(new_ref, ROWS, ROWS // HD), state, causal)

    def pair(i, state):
        wait_for(2 * i)
        wait_for(2 * i + 1)
        a, b = held.at[2 * i], held.at[2 * i + 1]
        keys = jnp.concatenate([a[:ROWS, :], b[:ROWS, :]], axis=0)
        cols = jnp.concatenate(
            [chunk_cols(a, ROWS, ROWS // HD), chunk_cols(b, ROWS, ROWS // HD)], axis=1
        )
        return direct(keys, cols, state)

    def single(i, state):
        wait_for(i)
        block = held.at[i]

        def seen(shape):
            return lax.broadcasted_iota(jnp.int32, shape, 0) + i * ROWS < live

        return direct(block[:ROWS, :], chunk_cols(block, ROWS, ROWS // HD), state, seen)

    pairs = live // (2 * ROWS)
    used = (live + ROWS - 1) // ROWS
    state = lax.fori_loop(0, pairs, pair, state)
    state = lax.fori_loop(2 * pairs, used, single, state)

    def drain(i, carry):
        wait_for(i)
        return carry

    lax.fori_loop(used, n_blocks, drain, 0)
    acc, total = state
    total = jnp.sum(total, axis=0, keepdims=True)

    def write(acc, total):
        out = jnp.transpose(acc / total).astype(jnp.bfloat16)
        for part in range(2):
            place = core if part == 0 else 1 - core
            for p in range(CHIPS):
                first = part * half + p * piece
                o_ref[p, place] = out[first : first + piece, :]

    write(acc, total)
    fine = jnp.logical_and(total > 2.0**-60, total < 2.0**110)
    bad = jnp.max(jnp.where(fine, 0, 1))

    @pl.when(bad > 0)
    def _():
        def careful(keys, cols, state, seen):
            top, total, acc = state
            s = jnp.where(seen, scores_of(keys), NEG)
            new_top = jnp.maximum(top, jnp.max(s, axis=0, keepdims=True))
            factor = jnp.exp2((top - new_top) * SCALE2)
            p = jnp.where(seen, jnp.exp2((s - new_top) * SCALE2), 0.0)
            total = total * factor + jnp.sum(p, axis=0, keepdims=True)
            return new_top, total, acc * factor + add_values(cols, p)

        def step(i, state):
            block = held.at[i]
            shape = (HD * 2, span)

            def inner(j, state):
                first = pl.multiple_of(j * 2 * HD, 2 * HD)
                row = lax.broadcasted_iota(jnp.int32, shape, 0) + first
                return careful(
                    block[pl.ds(first, 2 * HD), :],
                    chunk_cols(block, ROWS + first, 2),
                    state,
                    row + i * ROWS < live,
                )

            return lax.fori_loop(0, ROWS // (2 * HD), inner, state)

        def new_step(j, state):
            first = pl.multiple_of(j * 2 * HD, 2 * HD)
            row = lax.broadcasted_iota(jnp.int32, (2 * HD, span), 0) + first
            return careful(
                new_ref[pl.ds(first, 2 * HD), :],
                chunk_cols(new_ref, ROWS + first, 2),
                state,
                row <= query,
            )

        state = (
            jnp.full((1, span), NEG, jnp.float32),
            jnp.zeros((1, span), jnp.float32),
            jnp.zeros((HD, span), jnp.float32),
        )
        state = lax.fori_loop(0, used, step, state)
        _, total, acc = lax.fori_loop(0, ROWS // (2 * HD), new_step, state)
        write(acc, total)


def attention(meta, q, new, blocks):
    n = len(blocks)
    span = q.shape[0]
    vmem = pl.BlockSpec(memory_space=pltpu.VMEM)
    return pl.pallas_call(
        functools.partial(attention_kernel, n),
        in_specs=[pl.BlockSpec(memory_space=pltpu.SMEM), vmem, vmem]
        + [pl.BlockSpec(memory_space=pl.ANY)] * n,
        out_specs=vmem,
        out_shape=jax.ShapeDtypeStruct((CHIPS, NC, span // (CHIPS * NC), HD), jnp.bfloat16),
        scratch_shapes=[
            pltpu.VMEM((n, 2 * ROWS, HD), jnp.bfloat16),
            pltpu.SemaphoreType.DMA((n,)),
        ],
        compiler_params=pltpu.CompilerParams(vmem_limit_bytes=48 * 2**20),
        cost_estimate=pl.CostEstimate(
            flops=4 * span * HD * ROWS * (n + 1),
            bytes_accessed=2 * n * 2 * ROWS * HD,
            transcendentals=span * ROWS * (n + 1),
        ),
    )(meta, q, new, *blocks)


def on_device(
    tokens, q_weight, k_weight, v_weight, cache_keys, cache_values, cache_len, span_start
):
    n_tensor = lax.axis_size("tensor")
    me = lax.axis_index("ulysses")
    core = me % NC
    chip = me // NC
    own_rows = tokens.shape[0]
    width = q_weight.shape[1] // NC
    depth = q_weight.shape[0]

    mine = lax.all_to_all(
        tokens.reshape(own_rows, CHIPS, NC * depth),
        "ulysses",
        split_axis=1,
        concat_axis=0,
        axis_index_groups=SAME_CORE,
        tiled=True,
    ).reshape(CHIPS * own_rows, NC * depth)

    both = jnp.stack([k_weight, v_weight])
    keep = jnp.concatenate(
        [
            lax.dynamic_slice_in_dim(q_weight, core * width, width, 1),
            lax.dynamic_index_in_dim(both, core, 0, keepdims=False),
        ],
        axis=1,
    )
    give = jnp.concatenate(
        [
            lax.dynamic_slice_in_dim(q_weight, (1 - core) * width, width, 1),
            lax.dynamic_index_in_dim(both, 1 - core, 0, keepdims=False),
        ],
        axis=1,
    )
    got = hop(give, dc=1)
    weight = jnp.where(
        core == 0,
        jnp.concatenate([keep, got], axis=0),
        jnp.concatenate([got, keep], axis=0),
    )

    cols = jnp.transpose(cache_values.reshape(ROWS // HD, HD, HD), (0, 2, 1)).reshape(ROWS, HD)
    b000 = jnp.concatenate([cache_keys, cols], axis=0)
    b300 = hop(b000, dz=1)
    b100 = hop(b000, dz=-1)
    b010 = hop(b000, dx=1)
    b310 = hop(b010, dz=1)
    b200 = hop(b100, dz=-1)
    b110 = hop(b100, dx=1)
    b210 = hop(b200, dx=1)
    lineage = {
        (0, 0): b000, (1, 0): b100, (2, 0): b200, (3, 0): b300,
        (0, 1): b010, (1, 1): b110, (2, 1): b210, (3, 1): b310,
    }
    blocks, slots = [], []
    z_me, x_me = chip // NX, chip % NX
    for (dz, dx), block in lineage.items():
        place = ((z_me + dz) % NZ) * NX * NC + ((x_me + dx) % NX) * NC
        blocks += [block, hop(block, dc=1)]
        slots += [place + core, place + 1 - core]

    other = hop(mine, dc=1)
    spread = jnp.concatenate([mine, other], axis=0)
    span = spread.shape[0]
    heads = width // HD

    kv_part = jnp.dot(spread, weight[:, width:], preferred_element_type=jnp.float32)
    kv_parts = lax.all_to_all(
        kv_part.reshape(NC, CHIPS, own_rows, HD),
        "ulysses",
        split_axis=1,
        concat_axis=1,
        axis_index_groups=SAME_CORE,
        tiled=True,
    )
    kv_sum = jnp.sum(kv_parts, axis=1)
    kv_sum = jnp.where(core == 0, kv_sum, kv_sum[::-1]).reshape(NC * own_rows, HD)
    kv_pos = span_start[0] + chip * NC * own_rows + jnp.arange(NC * own_rows, dtype=jnp.int32)
    kv_angles = angle_table(kv_pos, HD)
    k_rot = rotate(kv_sum, jnp.cos(kv_angles), jnp.sin(kv_angles), 1)
    kv_own = jnp.where(core == 0, k_rot, kv_sum.T).astype(jnp.bfloat16)
    kv_all = lax.all_to_all(
        jnp.broadcast_to(kv_own[None], (CHIPS,) + kv_own.shape),
        "ulysses",
        split_axis=0,
        concat_axis=0,
        axis_index_groups=SAME_CORE,
        tiled=True,
    ).reshape(SPAN, HD)
    kv_other = hop(kv_all, dc=1)
    new = jnp.where(
        core == 0,
        jnp.concatenate([kv_all, kv_other], axis=0),
        jnp.concatenate([kv_other, kv_all], axis=0),
    )

    q_part = jnp.einsum(
        "td,dhk->htk",
        spread,
        weight[:, :width].reshape(NC * depth, heads, HD),
        preferred_element_type=jnp.float32,
    )
    q_parts = lax.all_to_all(
        (q_part * BOOST).astype(jnp.float16),
        "ulysses",
        split_axis=0,
        concat_axis=0,
        axis_index_groups=SAME_CORE,
        tiled=True,
    )
    q_sum = jnp.sum(q_parts.astype(jnp.float32), axis=0) * (1.0 / BOOST)
    row = jnp.arange(span, dtype=jnp.int32)
    half = span // 2
    own = jnp.where(row < half, core, 1 - core)
    inside = row % half
    index = (inside // own_rows) * NC * own_rows + own * own_rows + inside % own_rows
    angles = angle_table(span_start[0] + index, HD)
    q_rot = rotate(q_sum, jnp.cos(angles), jnp.sin(angles), 1).astype(jnp.bfloat16)

    meta = jnp.stack([cache_len[0], core] + slots).astype(jnp.int32)
    mixed = attention(meta, q_rot, new, blocks).reshape(span, HD)
    n_all = n_tensor * NC * CHIPS
    moved = lax.all_to_all(
        mixed.reshape(n_all, span // n_all, HD),
        ("tensor", "ulysses"),
        split_axis=0,
        concat_axis=0,
        tiled=True,
    )
    moved = moved.reshape(n_tensor, CHIPS, NC, span // n_all, HD)
    return jnp.transpose(moved, (3, 0, 2, 1, 4)).reshape(span // n_all, n_all * HD)


def solution(mesh):
    placed = (
        P("ulysses", None),
        P("ulysses", "tensor"),
        P("ulysses", "tensor"),
        P("ulysses", "tensor"),
        P("ulysses", "tensor"),
        P("ulysses", "tensor"),
        P(),
        P(),
    )
    return jax.shard_map(
        on_device,
        mesh=mesh,
        in_specs=placed,
        out_specs=P(("tensor", "ulysses"), None),
        check_vma=False,
    )
```

time: 524 us -> 260 us (0.50)
  waiting for transfers between devices: 364 us -> 58.5 us
  Pallas kernels: 0 us -> 67.4 us
  matrix products: 75.9 us -> 14.5 us
  starting transfers between devices: 9.45 us -> 51.2 us
  local copies, waits for them, and re-layouts: 11 us -> 23.9 us
  between operations: 13.9 us -> 1.6 us
  other arithmetic: 30.4 us -> 19.2 us
    psum x1 -> x0, waiting for transfers between devices: 125 us -> none  [on_device(): lax.psum(kv_part.astype(jnp.bfloat16), 'ulysses').astype(jnp.float32)]
    all_gather x2 -> x0, waiting for transfers between devices: 110 us -> none  [the longest x1 55.9 us: on_device(): values_piece = lax.all_gather(cache_values, 'ulysses', axis=0, tiled=True)]
    reduce_scatter x1 -> x0, waiting for transfers between devices: 105 us -> none  [on_device(): lax.psum_scatter(jnp.transpose(term, (1, 0, 2, 3)).reshape(q_cols // n_ul...]
    pallas_call x0 -> x1, Pallas kernels: none -> 67.4 us  [attention(): pl.pallas_call(functools.partial(attention_kernel, n), in_specs=[pl.Block...]
    dot_general x36 -> x2, matrix products: 75.9 us -> 14.5 us  [the longest x1 9.38 us: on_device(): jnp.einsum('td,dhk->htk', spread, weight[:, :width].reshape(NC * depth, h...]
    ppermute x0 -> x18, waiting for transfers between devices: none -> 36.5 us  [hop(): return lax.ppermute(values, 'ulysses', pairs)]
    ppermute x0 -> x18, starting transfers between devices: none -> 26 us  [hop(): return lax.ppermute(values, 'ulysses', pairs)]
    all_to_all x1 -> x4, starting transfers between devices: 9.29 us -> 25.2 us  [the longest x1 8.32 us: on_device(): lax.all_to_all(tokens.reshape(own_rows, CHIPS, NC * depth), 'ulysses', sp...]
  transfers between devices with their start and end apart: 5 -> 22, of which waited for: 5 -> 4; matrix products, arithmetic and copies ran while one was open for 4% -> 17% of each run, Pallas kernels for 0% -> 0%
where the time goes in v1:
time: 260 us; the launch traced here: 257 us
  Pallas kernels  67.4 us (26%)
  waiting for transfers between devices  58.5 us (22%)
  starting transfers between devices  51.2 us (20%)
  local copies, waits for them, and re-layouts  23.9 us (9%)
  blocking collectives  21.1 us (8%)
  other arithmetic  19.2 us (7%)
  matrix products  14.5 us (6%)
    pallas_call x1, Pallas kernels, attention(): pl.pallas_call(functools.partial(attention_kernel, n), in_specs=[pl.Block...  67.4 us
    ppermute x18, waiting for transfers between devices, hop(): return lax.ppermute(values, 'ulysses', pairs)  36.5 us
    ppermute x18, starting transfers between devices, hop(): return lax.ppermute(values, 'ulysses', pairs)  26 us
    all_to_all x1, waiting for transfers between devices, on_device(): lax.all_to_all(tokens.reshape(own_rows, CHIPS, NC * depth), 'ulysses', sp...  22.1 us
    all_to_all x1, blocking collectives, on_device(): lax.all_to_all(mixed.reshape(n_all, span // n_all, HD), ('tensor', 'ulyss...  21.1 us
    slice x2, local copies, waits for them, and re-layouts, on_device(): weight[:, :width].reshape(NC * depth, heads, HD)  11.2 us
    dot_general x1, matrix products, on_device(): jnp.einsum('td,dhk->htk', spread, weight[:, :width].reshape(NC * depth, h...  9.38 us
    select_n x1, other arithmetic, on_device(): jnp.where(core == 0, jnp.concatenate([keep, got], axis=0), jnp.concatenat...  9.21 us
  transfers between devices with their start and end apart: 22, of which 4 were waited for; matrix products, arithmetic and copies ran while one was open for 17% of the time, Pallas kernels for 0%

profile of v1, /device:TPU:1, one launch (start us, length us, event | category | flops | bytes accessed | tf_op | source)
XLA Modules:
  0.0 257.4 jit_solution(4659958226353959128)
XLA Ops:
  0.0 3.2 %copy.44 = bf16[8,8,8,2048]{3,2,0,1:T(8,128)(2,1)} copy(bf16[8,8,8,2048]{3,2,1,0:T(8,128)(2,1)} %bitcast.61) | data formatting | bytes 4194304 | tf_op jit(solution)/shard_map/reshape | solution.py:233
  3.2 8.3 %all-to-all-start = ((bf16[64,8,2048]{2,0,1:T(8,128)(2,1)}), bf16[64,8,2048]{2,0,1:T(8,128)(2,1)}, u32[]{:S(2)}, u32[]{:S(2)}) async-start(bf16[64,8,2048]{2,0,1:T(8,128)(2,1)} %bitcast.56), calls=%async_computation | async-start | bytes 4194304 | tf_op jit(solution)/shard_map/all_to_all | solution.py:232
  11.5 2.7 %constant_dynamic-slice_fusion.1 = (bf16[1024,1024]{1,0:T(8,128)(2,1)S(1)}, bf16[1024,1024]{1,0:T(8,128)(2,1)S(1)}) fusion(bf16[1024,2048]{1,0:T(8,128)(2,1)} %param.9, s32[]{:T(128)S(6)} %select_n.155, s32[]{:T(128)S(6)} %select_n.157), kind=kLoop, calls=%fused_computation.67 | loop fusion | bytes 8388616 | tf_op jit(solution)/shard_map/dynamic_slice | solution.py:244
  14.5 1.6 pad_maximum_fusion.3
  17.1 22.1 %all-to-all-done = bf16[64,8,2048]{2,0,1:T(8,128)(2,1)} async-done(((bf16[64,8,2048]{2,0,1:T(8,128)(2,1)}), bf16[64,8,2048]{2,0,1:T(8,128)(2,1)}, u32[]{:S(2)}, u32[]{:S(2)}) %all-to-all-start) | async-done | bytes 2097184 | tf_op jit(solution)/shard_map/all_to_all | solution.py:232
  39.2 1.9 collective-permute-start.1
  41.1 9.2 %maximum_select_fusion = bf16[2048,1152]{1,0:T(8,128)(2,1)S(1)} fusion(bf16[1024,1152]{1,0:T(8,128)(2,1)} %collective-permute-done, bf16[1024,128]{1,0:T(8,128)(2,1)S(1)} %get-tuple-element.9, bf16[1024,1024]{1,0:T(8,128)(2,1)S(1)} %get-tuple-element.5, pred[]{:T(512)S(6)} %eq.28), kind=kLoop, calls=%fused_computation | loop fusion | flops 30670848 | bytes 9437185 | tf_op jit(solution)/shard_map/jit(_where)/select_n | solution.py:257
  50.3 5.2 %fusion.2 = f32[1024,128]{1,0:T(8,128)S(1)} fusion(bf16[512,2048]{1,0:T(8,128)(2,1)} %collective-permute-done.1, bf16[512,2048]{1,0:T(8,128)(2,1)} %bitcast.24, bf16[2048,1152]{1,0:T(8,128)(2,1)S(1)} %maximum_select_fusion), kind=kOutput, calls=%fused_computation.6 | convolution fusion | flops 545259520 | bytes 5242880 | tf_op jit(solution)/shard_map/dot_general | solution.py:288
  56.3 3.5 %all-to-all-start.2 = ((f32[2,8,64,128]{3,2,0,1:T(8,128)}), f32[2,8,64,128]{3,2,0,1:T(8,128)S(1)}, u32[]{:S(2)}, u32[]{:S(2)}) async-start(f32[2,8,64,128]{3,2,0,1:T(8,128)} %copy.34), calls=%async_computation.2 | async-start | bytes 1048576 | tf_op jit(solution)/shard_map/all_to_all | solution.py:289
  60.5 4.6 %slice.8 = bf16[2048,1024]{1,0:T(8,128)(2,1)} slice(bf16[2048,1152]{1,0:T(8,128)(2,1)} %copy-done), slice={[0:2048], [0:1024]} | slice | bytes 8388608 | tf_op jit(solution)/shard_map/slice | solution.py:321
  65.2 6.6 %copy.30 = bf16[2048,1024]{0,1:T(8,128)(2,1)} copy(bf16[2048,1024]{1,0:T(8,128)(2,1)} %slice.8) | data formatting | bytes 8388608 | tf_op jit(solution)/shard_map/slice | solution.py:321
  73.1 6.6 %all-to-all-start.3 = ((bf16[8,128,128]{2,1,0:T(8,128)(2,1)}), bf16[8,128,128]{2,1,0:T(8,128)(2,1)S(1)}, u32[]{:S(2)}, u32[]{:S(2)}) async-start(bf16[8,128,128]{2,1,0:T(8,128)(2,1)} %broadcast_in_dim.20), calls=%async_computation.3 | async-start | bytes 524288 | tf_op jit(solution)/shard_map/all_to_all | solution.py:303
  79.7 9.4 %fusion.3 = f16[8,1024,128]{1,2,0:T(8,128)(2,1)} fusion(bf16[2048,8,128]{0,2,1:T(8,128)(2,1)} %bitcast.60, bf16[512,2048]{1,0:T(8,128)(2,1)} %collective-permute-done.1, bf16[512,2048]{1,0:T(8,128)(2,1)} %bitcast.24), kind=kOutput, calls=%fused_computation.8 | convolution fusion | flops 4305453056 | bytes 10485760 | tf_op jit(solution)/shard_map/td,dhk->htk/dot_general | solution.py:318
  89.1 6.8 %all-to-all-start.1 = ((f16[8,1024,128]{1,2,0:T(8,128)(2,1)}), f16[8,1024,128]{1,2,0:T(8,128)(2,1)}, u32[]{:S(2)}, u32[]{:S(2)}) async-start(f16[8,1024,128]{1,2,0:T(8,128)(2,1)} %fusion.3), calls=%async_computation.1 | async-start | bytes 4194304 | tf_op jit(solution)/shard_map/all_to_all | solution.py:324
  96.1 2.7 %collective-permute-start.4 = (bf16[2048,128]{1,0:T(8,128)(2,1)S(1)}, bf16[2048,128]{1,0:T(8,128)(2,1)S(1)}, u32[]{:S(2)}, u32[]{:S(2)}) collective-permute-start(bf16[2048,128]{1,0:T(8,128)(2,1)S(1)} %pad_maximum_fusion.4.rest_0_), channel_id=1, source_target_pairs={{0,12},{1,13},{2,14},{3,15},{4,0},{5,1},{6,2},{7,3},{8,4},{9,5},{1... | collective-permute-start | bytes 1572872 | tf_op jit(solution)/shard_map/ppermute | solution.py:45
  98.8 2.7 %collective-permute-start.10 = (bf16[2048,128]{1,0:T(8,128)(2,1)S(1)}, bf16[2048,128]{1,0:T(8,128)(2,1)S(1)}, u32[]{:S(2)}, u32[]{:S(2)}) collective-permute-start(bf16[2048,128]{1,0:T(8,128)(2,1)S(1)} %pad_maximum_fusion.4.rest_0_), channel_id=1, source_target_pairs={{0,2},{1,3},{2,0},{3,1},{4,6},{5,7},{6,4},{7,5},{8,10},{9,11},{10,... | collective-permute-start | bytes 1572872 | tf_op jit(solution)/shard_map/ppermute | solution.py:45
  101.5 2.0 collective-permute-start.3
  103.5 27.3 %collective-permute-done.4.rest_2_ = bf16[2048,128]{1,0:T(8,128)(2,1)S(1)} collective-permute-done((bf16[2048,128]{1,0:T(8,128)(2,1)S(1)}, bf16[2048,128]{1,0:T(8,128)(2,1)S(1)}, u32[]{:S(2)}, u32[]{:S(2)}) %collective-permute-start.4) | collective-permute-done | bytes 524320 | tf_op jit(solution)/shard_map/ppermute | solution.py:45
  130.8 1.5 collective-permute-start.6
  132.4 2.0 collective-permute-start.2
  135.1 2.8 %collective-permute-start.12 = (bf16[2048,128]{1,0:T(8,128)(2,1)S(1)}, bf16[2048,128]{1,0:T(8,128)(2,1)}, u32[]{:S(2)}, u32[]{:S(2)}) collective-permute-start(bf16[2048,128]{1,0:T(8,128)(2,1)S(1)} %collective-permute-done.4.rest_2_), channel_id=1, source_target_pairs={{0,2},{1,3},{2,0},{3,1},{4,6},{5,7},{6,4},{7,5},{8,10},{9,11},{10,... | collective-permute-start | bytes 1572872 | tf_op jit(solution)/shard_map/ppermute | solution.py:45
  138.4 3.9 %collective-permute-done.6.rest_4_ = bf16[2048,128]{1,0:T(8,128)(2,1)} collective-permute-done((bf16[2048,128]{1,0:T(8,128)(2,1)S(1)}, bf16[2048,128]{1,0:T(8,128)(2,1)}, u32[]{:S(2)}, u32[]{:S(2)}) %collective-permute-start.6) | collective-permute-done | bytes 524320 | tf_op jit(solution)/shard_map/ppermute | solution.py:45
  142.3 3.0 %collective-permute-start.11 = (bf16[2048,128]{1,0:T(8,128)(2,1)S(1)}, bf16[2048,128]{1,0:T(8,128)(2,1)}, u32[]{:S(2)}, u32[]{:S(2)}) collective-permute-start(bf16[2048,128]{1,0:T(8,128)(2,1)S(1)} %collective-permute-done.10.rest_8_), channel_id=1, source_target_pairs={{0,1},{1,0},{2,3},{3,2},{4,5},{5,4},{6,7},{7,6},{8,9},{9,8},{10,11... | collective-permute-start | bytes 1572872 | tf_op jit(solution)/shard_map/ppermute | solution.py:45
  145.3 4.3 %collective-permute-start.14 = (bf16[2048,128]{1,0:T(8,128)(2,1)}, bf16[2048,128]{1,0:T(8,128)(2,1)}, u32[]{:S(2)}, u32[]{:S(2)}) collective-permute-start(bf16[2048,128]{1,0:T(8,128)(2,1)} %collective-permute-done.6.rest_4_), channel_id=1, source_target_pairs={{0,2},{1,3},{2,0},{3,1},{4,6},{5,7},{6,4},{7,5},{8,10},{9,11},{10,... | collective-permute-start | bytes 1572872 | tf_op jit(solution)/shard_map/ppermute | solution.py:45
  149.6 1.2 maximum_select_fusion.1.new_ref
  150.8 2.9 %convert_reduce_fusion = f32[1024,128]{0,1:T(8,128)} fusion(f16[8,1024,128]{1,2,0:T(8,128)(2,1)} %all-to-all-done.1), kind=kLoop, calls=%fused_computation.4 | loop fusion | flops 1966080 | bytes 2621440 | tf_op jit(solution)/shard_map/reduce_sum | solution.py:332
  153.7 2.1 copy.32
  156.8 5.3 %collective-permute-done.14.rest_12_ = bf16[2048,128]{1,0:T(8,128)(2,1)} collective-permute-done((bf16[2048,128]{1,0:T(8,128)(2,1)}, bf16[2048,128]{1,0:T(8,128)(2,1)}, u32[]{:S(2)}, u32[]{:S(2)}) %collective-permute-start.14) | collective-permute-done | bytes 524320 | tf_op jit(solution)/shard_map/ppermute | solution.py:45
  162.7 1.1 broadcast_multiply_fusion
  163.8 2.4 fusion.11
  168.2 67.4 %shard_map.82 = bf16[8,2,64,128]{3,2,1,0:T(8,128)(2,1)S(1)} custom-call(s32[18]{0:T(128)S(1)} %stack.80.meta, bf16[1024,128]{1,0:T(8,128)(2,1)S(1)} %pad_maximum_fusion.5.q_ref, bf16[2048,128]{1,0:T(8,128)(2,1)S(1)} %maximum_select_fusion.1.new_ref, bf16[2048,128]{1,0:T(8,128)(2,1)S(1)} %pad_maximum_fusion.4.rest_0_, ...), custom_call_target="tpu_custom_call" | custom-call | flops 9126805504 | bytes 8388608 | tf_op jit(solution)/shard_map/pallas_call | solution.py:202
  235.5 21.1 %all_to_all.35 = bf16[128,8,128]{2,1,0:T(8,128)(2,1)S(1)} all-to-all(bf16[128,8,128]{2,1,0:T(8,128)(2,1)S(1)} %bitcast.59), channel_id=1, replica_groups=mesh['tensor'=8,'ulysses'=16] {'tensor','ulysses'}, dimensions={0} | all-to-all | bytes 524288 | tf_op jit(solution)/shard_map/all_to_all | solution.py:344
  (64 shorter events, 8.6 us)
Async XLA Ops:
  3.2 36.0 %all-to-all-start = ((bf16[64,8,2048]{2,0,1:T(8,128)(2,1)}), bf16[64,8,2048]{2,0,1:T(8,128)(2,1)}, u32[]{:S(2)}, u32[]{:S(2)}) async-start(bf16[64,8,2048]{2,0,1:T(8,128)(2,1)} %bitcast.56), calls=%async_computation | async-start | bytes 4194304 | tf_op jit(solution)/shard_map/all_to_all | solution.py:232
  11.5 2.7 %copy-start.1 = (bf16[1024,128]{1,0:T(8,128)(2,1)S(1)}, bf16[1024,128]{1,0:T(8,128)(2,1)}, u32[]{:S(2)}) copy-start(bf16[1024,128]{1,0:T(8,128)(2,1)} %param.10) | copy-start | bytes 786436
  11.5 2.8 %copy-start.2 = (bf16[1024,128]{1,0:T(8,128)(2,1)S(1)}, bf16[1024,128]{1,0:T(8,128)(2,1)}, u32[]{:S(2)}) copy-start(bf16[1024,128]{1,0:T(8,128)(2,1)} %param.11) | copy-start | bytes 786436
  16.1 24.9 %collective-permute-start = (bf16[1024,1152]{1,0:T(8,128)(2,1)}, bf16[1024,1152]{1,0:T(8,128)(2,1)}, u32[]{:S(2)}, u32[]{:S(2)}) collective-permute-start(bf16[1024,1152]{1,0:T(8,128)(2,1)} %pad_maximum_fusion.3), channel_id=1, source_target_pairs={{0,1},{1,0},{2,3},{3,2},{4,5},{5,4},{6,7},{7,6},{8,9},{9,8},{10,11... | collective-permute-start | bytes 7077896 | tf_op jit(solution)/shard_map/ppermute | solution.py:45
  39.2 11.1 %collective-permute-start.1 = (bf16[512,2048]{1,0:T(8,128)(2,1)}, bf16[512,2048]{1,0:T(8,128)(2,1)}, u32[]{:S(2)}, u32[]{:S(2)}) collective-permute-start(bf16[512,2048]{1,0:T(8,128)(2,1)} %bitcast.24), channel_id=1, source_target_pairs={{0,1},{1,0},{2,3},{3,2},{4,5},{5,4},{6,7},{7,6},{8,9},{9,8},{10,11... | collective-permute-start | bytes 6291464 | tf_op jit(solution)/shard_map/ppermute | solution.py:45
  50.3 5.2 %copy-start = (bf16[2048,1152]{1,0:T(8,128)(2,1)}, bf16[2048,1152]{1,0:T(8,128)(2,1)S(1)}, u32[]{:S(2)}) copy-start(bf16[2048,1152]{1,0:T(8,128)(2,1)S(1)} %maximum_select_fusion) | copy-start | bytes 14155780
  56.3 15.4 %all-to-all-start.2 = ((f32[2,8,64,128]{3,2,0,1:T(8,128)}), f32[2,8,64,128]{3,2,0,1:T(8,128)S(1)}, u32[]{:S(2)}, u32[]{:S(2)}) async-start(f32[2,8,64,128]{3,2,0,1:T(8,128)} %copy.34), calls=%async_computation.2 | async-start | bytes 1048576 | tf_op jit(solution)/shard_map/all_to_all | solution.py:289
  73.1 16.0 %all-to-all-start.3 = ((bf16[8,128,128]{2,1,0:T(8,128)(2,1)}), bf16[8,128,128]{2,1,0:T(8,128)(2,1)S(1)}, u32[]{:S(2)}, u32[]{:S(2)}) async-start(bf16[8,128,128]{2,1,0:T(8,128)(2,1)} %broadcast_in_dim.20), calls=%async_computation.3 | async-start | bytes 524288 | tf_op jit(solution)/shard_map/all_to_all | solution.py:303
  89.1 6.8 %copy-start.3 = (bf16[1024,128]{1,0:T(8,128)(2,1)S(1)}, bf16[1024,128]{1,0:T(8,128)(2,1)}, u32[]{:S(2)}) copy-start(bf16[1024,128]{1,0:T(8,128)(2,1)} %param.13) | copy-start | bytes 786436
  89.1 7.0 %copy-start.4 = (bf16[1024,128]{1,0:T(8,128)(2,1)S(1)}, bf16[1024,128]{1,0:T(8,128)(2,1)}, u32[]{:S(2)}) copy-start(bf16[1024,128]{1,0:T(8,128)(2,1)} %param.12) | copy-start | bytes 786436
  89.1 61.7 %all-to-all-start.1 = ((f16[8,1024,128]{1,2,0:T(8,128)(2,1)}), f16[8,1024,128]{1,2,0:T(8,128)(2,1)}, u32[]{:S(2)}, u32[]{:S(2)}) async-start(f16[8,1024,128]{1,2,0:T(8,128)(2,1)} %fusion.3), calls=%async_computation.1 | async-start | bytes 4194304 | tf_op jit(solution)/shard_map/all_to_all | solution.py:324
  96.1 34.7 %collective-permute-start.4 = (bf16[2048,128]{1,0:T(8,128)(2,1)S(1)}, bf16[2048,128]{1,0:T(8,128)(2,1)S(1)}, u32[]{:S(2)}, u32[]{:S(2)}) collective-permute-start(bf16[2048,128]{1,0:T(8,128)(2,1)S(1)} %pad_maximum_fusion.4.rest_0_), channel_id=1, source_target_pairs={{0,12},{1,13},{2,14},{3,15},{4,0},{5,1},{6,2},{7,3},{8,4},{9,5},{1... | collective-permute-start | bytes 1572872 | tf_op jit(solution)/shard_map/ppermute | solution.py:45
  98.8 36.3 %collective-permute-start.10 = (bf16[2048,128]{1,0:T(8,128)(2,1)S(1)}, bf16[2048,128]{1,0:T(8,128)(2,1)S(1)}, u32[]{:S(2)}, u32[]{:S(2)}) collective-permute-start(bf16[2048,128]{1,0:T(8,128)(2,1)S(1)} %pad_maximum_fusion.4.rest_0_), channel_id=1, source_target_pairs={{0,2},{1,3},{2,0},{3,1},{4,6},{5,7},{6,4},{7,5},{8,10},{9,11},{10,... | collective-permute-start | bytes 1572872 | tf_op jit(solution)/shard_map/ppermute | solution.py:45
  101.5 36.4 %collective-permute-start.8 = (bf16[2048,128]{1,0:T(8,128)(2,1)S(1)}, bf16[2048,128]{1,0:T(8,128)(2,1)S(1)}, u32[]{:S(2)}, u32[]{:S(2)}) collective-permute-start(bf16[2048,128]{1,0:T(8,128)(2,1)S(1)} %pad_maximum_fusion.4.rest_0_), channel_id=1, source_target_pairs={{0,4},{1,5},{2,6},{3,7},{4,8},{5,9},{6,10},{7,11},{8,12},{9,13},{1... | collective-permute-start | bytes 1572872 | tf_op jit(solution)/shard_map/ppermute | solution.py:45
  101.5 36.7 %collective-permute-start.3 = (bf16[2048,128]{1,0:T(8,128)(2,1)S(1)}, bf16[2048,128]{1,0:T(8,128)(2,1)S(1)}, u32[]{:S(2)}, u32[]{:S(2)}) collective-permute-start(bf16[2048,128]{1,0:T(8,128)(2,1)S(1)} %pad_maximum_fusion.4.rest_0_), channel_id=1, source_target_pairs={{0,1},{1,0},{2,3},{3,2},{4,5},{5,4},{6,7},{7,6},{8,9},{9,8},{10,11... | collective-permute-start | bytes 1572872 | tf_op jit(solution)/shard_map/ppermute | solution.py:45
  130.8 11.5 %collective-permute-start.6 = (bf16[2048,128]{1,0:T(8,128)(2,1)S(1)}, bf16[2048,128]{1,0:T(8,128)(2,1)}, u32[]{:S(2)}, u32[]{:S(2)}) collective-permute-start(bf16[2048,128]{1,0:T(8,128)(2,1)S(1)} %collective-permute-done.4.rest_2_), channel_id=1, source_target_pairs={{0,12},{1,13},{2,14},{3,15},{4,0},{5,1},{6,2},{7,3},{8,4},{9,5},{1... | collective-permute-start | bytes 1572872 | tf_op jit(solution)/shard_map/ppermute | solution.py:45
  132.4 12.9 %collective-permute-start.2 = (bf16[1024,128]{1,0:T(8,128)(2,1)S(1)}, bf16[1024,128]{1,0:T(8,128)(2,1)S(1)}, u32[]{:S(2)}, u32[]{:S(2)}) collective-permute-start(bf16[1024,128]{1,0:T(8,128)(2,1)S(1)} %bitcast.64), channel_id=1, source_target_pairs={{0,1},{1,0},{2,3},{3,2},{4,5},{5,4},{6,7},{7,6},{8,9},{9,8},{10,11... | collective-permute-start | bytes 786440 | tf_op jit(solution)/shard_map/ppermute | solution.py:45
  135.1 20.6 %collective-permute-start.12 = (bf16[2048,128]{1,0:T(8,128)(2,1)S(1)}, bf16[2048,128]{1,0:T(8,128)(2,1)}, u32[]{:S(2)}, u32[]{:S(2)}) collective-permute-start(bf16[2048,128]{1,0:T(8,128)(2,1)S(1)} %collective-permute-done.4.rest_2_), channel_id=1, source_target_pairs={{0,2},{1,3},{2,0},{3,1},{4,6},{5,7},{6,4},{7,5},{8,10},{9,11},{10,... | collective-permute-start | bytes 1572872 | tf_op jit(solution)/shard_map/ppermute | solution.py:45
  137.9 18.4 %collective-permute-start.5 = (bf16[2048,128]{1,0:T(8,128)(2,1)S(1)}, bf16[2048,128]{1,0:T(8,128)(2,1)}, u32[]{:S(2)}, u32[]{:S(2)}) collective-permute-start(bf16[2048,128]{1,0:T(8,128)(2,1)S(1)} %collective-permute-done.4.rest_2_), channel_id=1, source_target_pairs={{0,1},{1,0},{2,3},{3,2},{4,5},{5,4},{6,7},{7,6},{8,9},{9,8},{10,11... | collective-permute-start | bytes 1572872 | tf_op jit(solution)/shard_map/ppermute | solution.py:45
  138.2 17.9 %collective-permute-start.16 = (bf16[2048,128]{1,0:T(8,128)(2,1)S(1)}, bf16[2048,128]{1,0:T(8,128)(2,1)}, u32[]{:S(2)}, u32[]{:S(2)}) collective-permute-start(bf16[2048,128]{1,0:T(8,128)(2,1)S(1)} %collective-permute-done.10.rest_8_), channel_id=1, source_target_pairs={{0,4},{1,5},{2,6},{3,7},{4,8},{5,9},{6,10},{7,11},{8,12},{9,13},{1... | collective-permute-start | bytes 1572872 | tf_op jit(solution)/shard_map/ppermute | solution.py:45
  142.3 14.3 %collective-permute-start.11 = (bf16[2048,128]{1,0:T(8,128)(2,1)S(1)}, bf16[2048,128]{1,0:T(8,128)(2,1)}, u32[]{:S(2)}, u32[]{:S(2)}) collective-permute-start(bf16[2048,128]{1,0:T(8,128)(2,1)S(1)} %collective-permute-done.10.rest_8_), channel_id=1, source_target_pairs={{0,1},{1,0},{2,3},{3,2},{4,5},{5,4},{6,7},{7,6},{8,9},{9,8},{10,11... | collective-permute-start | bytes 1572872 | tf_op jit(solution)/shard_map/ppermute | solution.py:45
  145.3 4.3 %copy-start.5 = (bf16[1024,128]{1,0:T(8,128)(2,1)}, bf16[1024,128]{1,0:T(8,128)(2,1)S(1)}, u32[]{:S(2)}) copy-start(bf16[1024,128]{1,0:T(8,128)(2,1)S(1)} %collective-permute-done.2) | copy-start | bytes 786436
  145.3 16.8 %collective-permute-start.14 = (bf16[2048,128]{1,0:T(8,128)(2,1)}, bf16[2048,128]{1,0:T(8,128)(2,1)}, u32[]{:S(2)}, u32[]{:S(2)}) collective-permute-start(bf16[2048,128]{1,0:T(8,128)(2,1)} %collective-permute-done.6.rest_4_), channel_id=1, source_target_pairs={{0,2},{1,3},{2,0},{3,1},{4,6},{5,7},{6,4},{7,5},{8,10},{9,11},{10,... | collective-permute-start | bytes 1572872 | tf_op jit(solution)/shard_map/ppermute | solution.py:45
  155.8 10.6 %collective-permute-start.9 = (bf16[2048,128]{1,0:T(8,128)(2,1)S(1)}, bf16[2048,128]{1,0:T(8,128)(2,1)S(1)}, u32[]{:S(2)}, u32[]{:S(2)}) collective-permute-start(bf16[2048,128]{1,0:T(8,128)(2,1)S(1)} %collective-permute-done.8.rest_6_), channel_id=1, source_target_pairs={{0,1},{1,0},{2,3},{3,2},{4,5},{5,4},{6,7},{7,6},{8,9},{9,8},{10,11... | collective-permute-start | bytes 1572872 | tf_op jit(solution)/shard_map/ppermute | solution.py:45
  156.1 10.3 %collective-permute-start.7 = (bf16[2048,128]{1,0:T(8,128)(2,1)}, bf16[2048,128]{1,0:T(8,128)(2,1)S(1)}, u32[]{:S(2)}, u32[]{:S(2)}) collective-permute-start(bf16[2048,128]{1,0:T(8,128)(2,1)} %collective-permute-done.6.rest_4_), channel_id=1, source_target_pairs={{0,1},{1,0},{2,3},{3,2},{4,5},{5,4},{6,7},{7,6},{8,9},{9,8},{10,11... | collective-permute-start | bytes 1572872 | tf_op jit(solution)/shard_map/ppermute | solution.py:45
  156.3 10.1 %collective-permute-start.13 = (bf16[2048,128]{1,0:T(8,128)(2,1)}, bf16[2048,128]{1,0:T(8,128)(2,1)S(1)}, u32[]{:S(2)}, u32[]{:S(2)}) collective-permute-start(bf16[2048,128]{1,0:T(8,128)(2,1)} %collective-permute-done.12.rest_10_), channel_id=1, source_target_pairs={{0,1},{1,0},{2,3},{3,2},{4,5},{5,4},{6,7},{7,6},{8,9},{9,8},{10,11... | collective-permute-start | bytes 1572872 | tf_op jit(solution)/shard_map/ppermute | solution.py:45
  156.6 9.8 %collective-permute-start.17 = (bf16[2048,128]{1,0:T(8,128)(2,1)}, bf16[2048,128]{1,0:T(8,128)(2,1)S(1)}, u32[]{:S(2)}, u32[]{:S(2)}) collective-permute-start(bf16[2048,128]{1,0:T(8,128)(2,1)} %collective-permute-done.16.rest_14_), channel_id=1, source_target_pairs={{0,1},{1,0},{2,3},{3,2},{4,5},{5,4},{6,7},{7,6},{8,9},{9,8},{10,11... | collective-permute-start | bytes 1572872 | tf_op jit(solution)/shard_map/ppermute | solution.py:45
  162.1 4.4 %collective-permute-start.15 = (bf16[2048,128]{1,0:T(8,128)(2,1)}, bf16[2048,128]{1,0:T(8,128)(2,1)S(1)}, u32[]{:S(2)}, u32[]{:S(2)}) collective-permute-start(bf16[2048,128]{1,0:T(8,128)(2,1)} %collective-permute-done.14.rest_12_), channel_id=1, source_target_pairs={{0,1},{1,0},{2,3},{3,2},{4,5},{5,4},{6,7},{7,6},{8,9},{9,8},{10,11... | collective-permute-start | bytes 1572872 | tf_op jit(solution)/shard_map/ppermute | solution.py:45
  166.4 0.8 copy-start.6
  166.4 1.0 copy-start.7
  167.4 0.8 copy-start.8

commit v2 on v0

v2 whole, which is shorter than its diff:
```python
import functools
import math

import jax
import jax.numpy as jnp
from jax import lax
from jax.experimental import pallas as pl
from jax.experimental.pallas import tpu as pltpu
from jax.sharding import PartitionSpec as P

HD = 128
NZ, NX, NC = 4, 2, 2
CHIPS = NZ * NX
NY = 4
META = 3
SPAN = 1024
ROWS = 1024
SCALE2 = math.log2(math.e) / math.sqrt(HD)
BOOST = 64.0
LOW = 2048.0
NEG = -1e30


def angle_table(positions, head_size):
    steps = jnp.arange(head_size // 2).astype(jnp.float32)
    freq = jnp.exp(-(2.0 * steps / head_size) * math.log(500000.0))
    return positions.astype(jnp.float32)[:, None] * freq[None, :]


def rotate(values, cos_t, sin_t, axis):
    first, second = jnp.split(values, 2, axis=axis)
    return jnp.concatenate(
        [first * cos_t - second * sin_t, second * cos_t + first * sin_t], axis=axis
    )


def unit(z, x, c):
    return (z % NZ) * NX * NC + (x % NX) * NC + c % NC


def hop(values, dz=0, dx=0, dc=0):
    pairs = [
        (unit(z, x, c), unit(z + dz, x + dx, c + dc))
        for z in range(NZ)
        for x in range(NX)
        for c in range(NC)
    ]
    return lax.ppermute(values, "ulysses", pairs)


def hop_y(values, dy):
    pairs = [(x * NY + y, x * NY + (y + dy) % NY) for x in range(2) for y in range(NY)]
    return lax.ppermute(values, "tensor", pairs)


SAME_CORE = [[NC * p + c for p in range(CHIPS)] for c in range(NC)]


def chunk_cols(block, first, count):
    parts = [block[pl.ds(first + HD * i, HD), :] for i in range(count)]
    return jnp.concatenate(parts, axis=1)


def trans_dot(keys, q):
    return lax.dot_general(keys, q, (((1,), (1,)), ((), ())), preferred_element_type=jnp.float32)


def add_values(cols, p):
    return lax.dot_general(
        cols, p.astype(jnp.bfloat16), (((1,), (0,)), ((), ())), preferred_element_type=jnp.float32
    )


def direct(q, keys, cols, state, seen=None):
    acc, total = state
    p = jnp.exp2(trans_dot(keys, q) * SCALE2)
    if seen is not None:
        p = jnp.where(seen(p.shape), p, 0.0)
    folded = jnp.sum(p.reshape(p.shape[0] // 8, 8, p.shape[1]), axis=0)
    return acc + add_values(cols, p), total + folded


def load_cache(pieces, places, meta, held, sems):
    for ref, (slot, first) in zip(pieces, places):
        place = meta[META + slot]
        rows = ref.shape[0]
        pltpu.make_async_copy(ref, held.at[place, pl.ds(first, rows)], sems.at[place]).start()


def turned(q_ref, cos_ref, sin_ref):
    raw = q_ref[...]
    turned_q = raw * cos_ref[...] + pltpu.roll(raw, HD // 2, 1) * sin_ref[...]
    return turned_q.astype(jnp.bfloat16)


def over_cache(q, live, held, sems, state):
    def wait_for(slot):
        pltpu.make_async_copy(held.at[slot], held.at[slot], sems.at[slot]).wait()

    def pair(i, state):
        wait_for(2 * i)
        wait_for(2 * i + 1)
        a, b = held.at[2 * i], held.at[2 * i + 1]
        keys = jnp.concatenate([a[:ROWS, :], b[:ROWS, :]], axis=0)
        cols = jnp.concatenate(
            [chunk_cols(a, ROWS, ROWS // HD), chunk_cols(b, ROWS, ROWS // HD)], axis=1
        )
        return direct(q, keys, cols, state)

    def single(i, state):
        wait_for(i)
        block = held.at[i]

        def seen(shape):
            return lax.broadcasted_iota(jnp.int32, shape, 0) + i * ROWS < live

        return direct(q, block[:ROWS, :], chunk_cols(block, ROWS, ROWS // HD), state, seen)

    def drain(i, carry):
        wait_for(i)
        return carry

    pairs = live // (2 * ROWS)
    used = (live + ROWS - 1) // ROWS
    state = lax.fori_loop(0, pairs, pair, state)
    state = lax.fori_loop(2 * pairs, used, single, state)
    lax.fori_loop(used, held.shape[0], drain, 0)
    return state


def empty_state(span):
    return jnp.zeros((HD, span), jnp.float32), jnp.zeros((8, span), jnp.float32)


def first_kernel(places, meta, q_ref, cos_ref, sin_ref, *rest):
    pieces = rest[: len(places)]
    acc_ref, total_ref, turned_ref, held, sems = rest[len(places) :]
    load_cache(pieces, places, meta, held, sems)
    q = turned(q_ref, cos_ref, sin_ref)
    turned_ref[...] = q
    acc, total = over_cache(q, meta[0], held, sems, empty_state(q.shape[0]))
    acc_ref[...] = acc
    total_ref[...] = total


def last_kernel(places, meta, acc_a, total_a, turned_a, acc_b, total_b, turned_b, new_ref, *rest):
    pieces = rest[: len(places)]
    o_ref, held, sems = rest[len(places) :]
    live, core, parity = meta[0], meta[1], meta[2]
    span = turned_a.shape[0]
    part = span // NC
    piece = part // CHIPS

    col = lax.broadcasted_iota(jnp.int32, (1, span), 1)
    kind = jnp.where(col < part, core, 1 - core)
    inside = col % part
    base = (inside // piece) * (4 * piece) + kind * (2 * piece) + inside % piece
    query_a, query_b = base + parity * piece, base + (1 - parity) * piece

    def before(query):
        return lambda shape: lax.broadcasted_iota(jnp.int32, shape, 0) <= query

    new_keys = jnp.concatenate([new_ref[NC * p] for p in range(CHIPS)], axis=0)
    new_cols = jnp.concatenate([new_ref[NC * p + 1] for p in range(CHIPS)], axis=1)
    q_a = turned_a[...]
    state_a = direct(q_a, new_keys, new_cols, (acc_a[...], total_a[...]), before(query_a))
    q_b = turned_b[...]
    state_b = direct(q_b, new_keys, new_cols, (acc_b[...], total_b[...]), before(query_b))

    def write(acc, total, sub):
        out = jnp.transpose(acc / total).astype(jnp.bfloat16)
        for k in range(NC):
            place = core if k == 0 else 1 - core
            for p in range(CHIPS):
                first = k * part + p * piece
                o_ref[p, place, sub] = out[first : first + piece, :]

    def is_bad(total):
        fine = jnp.logical_and(total > 2.0**-60, total < 2.0**110)
        return jnp.max(jnp.where(fine, 0, 1))

    def finish(state, sub):
        acc, total = state
        total = jnp.sum(total, axis=0, keepdims=True)
        write(acc, total, sub)
        return is_bad(total)

    def recompute(q, query, sub):
        def careful(keys, cols, state, seen):
            top, total, acc = state
            s = jnp.where(seen, trans_dot(keys, q), NEG)
            new_top = jnp.maximum(top, jnp.max(s, axis=0, keepdims=True))
            factor = jnp.exp2((top - new_top) * SCALE2)
            p = jnp.where(seen, jnp.exp2((s - new_top) * SCALE2), 0.0)
            total = total * factor + jnp.sum(p, axis=0, keepdims=True)
            return new_top, total, acc * factor + add_values(cols, p)

        def rows_from(first):
            return lax.broadcasted_iota(jnp.int32, (2 * HD, span), 0) + first

        def step(i, state):
            block = held.at[i]

            def inner(j, state):
                first = pl.multiple_of(j * 2 * HD, 2 * HD)
                keys = block[pl.ds(first, 2 * HD), :]
                cols = chunk_cols(block, ROWS + first, 2)
                return careful(keys, cols, state, rows_from(first) + i * ROWS < live)

            return lax.fori_loop(0, ROWS // (2 * HD), inner, state)

        def new_step(j, state):
            first = 2 * NC * j
            keys = jnp.concatenate([new_ref[first], new_ref[first + NC]], axis=0)
            cols = jnp.concatenate([new_ref[first + 1], new_ref[first + NC + 1]], axis=1)
            return careful(keys, cols, state, rows_from(j * 2 * HD) <= query)

        state = (
            jnp.full((1, span), NEG, jnp.float32),
            jnp.zeros((1, span), jnp.float32),
            jnp.zeros((HD, span), jnp.float32),
        )
        state = lax.fori_loop(0, (live + ROWS - 1) // ROWS, step, state)
        _, total, acc = lax.fori_loop(0, ROWS // (2 * HD), new_step, state)
        write(acc, total, sub)

    bad = jnp.maximum(finish(state_a, parity), finish(state_b, 1 - parity))

    @pl.when(bad > 0)
    def _():
        load_cache(pieces, places, meta, held, sems)

        def drain(i, carry):
            pltpu.make_async_copy(held.at[i], held.at[i], sems.at[i]).wait()
            return carry

        lax.fori_loop(0, held.shape[0], drain, 0)
        recompute(q_a, query_a, parity)
        recompute(q_b, query_b, 1 - parity)


def attention_call(kernel, meta, arrays, pieces, places, out_shape):
    span = SPAN // 2
    n = NC * CHIPS
    vmem = pl.BlockSpec(memory_space=pltpu.VMEM)
    return pl.pallas_call(
        functools.partial(kernel, places),
        in_specs=[pl.BlockSpec(memory_space=pltpu.SMEM)]
        + [vmem] * len(arrays)
        + [pl.BlockSpec(memory_space=pl.ANY)] * len(pieces),
        out_specs=jax.tree.map(lambda _: vmem, out_shape),
        out_shape=out_shape,
        scratch_shapes=[
            pltpu.VMEM((n, 2 * ROWS, HD), jnp.bfloat16),
            pltpu.SemaphoreType.DMA((n,)),
        ],
        compiler_params=pltpu.CompilerParams(vmem_limit_bytes=60 * 2**20),
        cost_estimate=pl.CostEstimate(
            flops=4 * span * HD * ROWS * (n + 1),
            bytes_accessed=2 * n * 2 * ROWS * HD,
            transcendentals=span * ROWS * (n + 1),
        ),
    )(meta, *arrays, *pieces)


def project_kernel(n_parts, meta, *rest):
    parts = rest[:n_parts]
    w_own, w_got, k_own, v_own, kv_got, o_ref, x_ref, kv_ref = rest[n_parts:]
    depth = w_own.shape[0]
    core = meta[0]
    own = pl.ds(pl.multiple_of(core * depth, depth), depth)
    got = pl.ds(pl.multiple_of((1 - core) * depth, depth), depth)

    def times(own_cols, got_cols):
        out = jnp.dot(x_ref[:, own], own_cols, preferred_element_type=jnp.float32)
        out += jnp.dot(x_ref[:, got], got_cols, preferred_element_type=jnp.float32)
        return out * BOOST

    @pl.when(pl.program_id(0) == 0)
    def _():
        first = 0
        for part in parts:
            x_ref[pl.ds(first, part.shape[0]), :] = part[...]
            first += part.shape[0]
        kv_ref[...] = times(jnp.where(core == 0, k_own[...], v_own[...]), kv_got[...])

    out = times(w_own[...], w_got[...])
    heads, span = o_ref.shape[0], x_ref.shape[0]
    kind = span // NC
    few = kind // CHIPS
    for h in range(heads):
        o_ref[h, :span, :] = out[:, h * HD : (h + 1) * HD]
        chip = pl.program_id(0) * heads + h
        for k in range(NC):
            value = kv_ref[pl.ds(pl.multiple_of(k * kind + chip * few, few), few), :]
            wide = value * 8193.0
            high = wide - (wide - value)
            high = jnp.where(jnp.abs(value) < 2.0**-14, 0.0, high)
            o_ref[h, pl.ds(span + k * few, few), :] = high
            o_ref[h, pl.ds(span + (NC + k) * few, few), :] = (value - high) * LOW


def project(core, parts, q_weight, k_weight, v_weight, got):
    depth, width = q_weight.shape[0], q_weight.shape[1] // NC
    span = sum(part.shape[0] for part in parts)
    tile = 2 * HD
    steps = width // tile
    rows = span + 2 * span // CHIPS
    whole = lambda n, m: (0, 0)
    return pl.pallas_call(
        functools.partial(project_kernel, len(parts)),
        grid_spec=pltpu.PrefetchScalarGridSpec(
            num_scalar_prefetch=1,
            grid=(steps,),
            in_specs=[pl.BlockSpec(part.shape, whole) for part in parts]
            + [
                pl.BlockSpec((depth, tile), lambda n, m: (0, m[0] * steps + n)),
                pl.BlockSpec((depth, tile), lambda n, m: (0, n)),
                pl.BlockSpec((depth, HD), whole),
                pl.BlockSpec((depth, HD), whole),
                pl.BlockSpec((depth, HD), whole),
            ],
            out_specs=pl.BlockSpec((tile // HD, rows, HD), lambda n, m: (n, 0, 0)),
            scratch_shapes=[
                pltpu.VMEM((span, NC * depth), jnp.bfloat16),
                pltpu.VMEM((span, HD), jnp.float32),
            ],
        ),
        out_shape=jax.ShapeDtypeStruct((width // HD, rows, HD), jnp.float32),
        compiler_params=pltpu.CompilerParams(vmem_limit_bytes=24 * 2**20),
        cost_estimate=pl.CostEstimate(
            flops=4 * span * depth * width,
            bytes_accessed=4 * span * depth + 4 * depth * width + 4 * span * width,
            transcendentals=0,
        ),
    )(core[None], *parts, q_weight, got[0], k_weight, v_weight, got[1])


def settle_kernel(meta, kv_a, kv_b, cos_ref, sin_ref, o_ref, rows):
    core, parity = meta[0], meta[1]
    few = kv_a.shape[1]
    for sub, kv in ((parity, kv_a), (1 - parity, kv_b)):
        for k, kind in enumerate((core, 1 - core)):
            first = pl.multiple_of((2 * kind + sub) * few, few)
            rows[pl.ds(first, few), :] = kv[k]
    value = rows[...]
    key = value * cos_ref[...] + pltpu.roll(value, HD // 2, 1) * sin_ref[...]
    out = jnp.where(core == 0, key, jnp.transpose(value)).astype(jnp.bfloat16)
    for i in range(o_ref.shape[0]):
        o_ref[i] = out


def settle(core, parity, kv_a, kv_b, cos_t, sin_t):
    vmem = pl.BlockSpec(memory_space=pltpu.VMEM)
    return pl.pallas_call(
        settle_kernel,
        in_specs=[pl.BlockSpec(memory_space=pltpu.SMEM)] + [vmem] * 4,
        out_specs=vmem,
        out_shape=jax.ShapeDtypeStruct((NC * CHIPS, HD, HD), jnp.bfloat16),
        scratch_shapes=[pltpu.VMEM((HD, HD), jnp.float32)],
    )(jnp.stack([core, parity]), kv_a, kv_b, cos_t, sin_t)


def tables(positions):
    angles = angle_table(positions, HD)
    cos_t, sin_t = jnp.cos(angles), jnp.sin(angles)
    return jnp.concatenate([cos_t, cos_t], axis=1), jnp.concatenate([-sin_t, sin_t], axis=1)


def trade(values, axis):
    return lax.all_to_all(
        values,
        "ulysses",
        split_axis=axis,
        concat_axis=axis,
        axis_index_groups=SAME_CORE,
        tiled=True,
    )


def on_device(
    tokens, q_weight, k_weight, v_weight, cache_keys, cache_values, cache_len, span_start
):
    barrier = lax.optimization_barrier
    n_tensor = lax.axis_size("tensor")
    me = lax.axis_index("ulysses").astype(jnp.int32)
    core = me % NC
    chip = me // NC
    parity = lax.axis_index("tensor").astype(jnp.int32) % 2
    own_rows, features = tokens.shape
    few = own_rows // 2
    depth, width = q_weight.shape[0], q_weight.shape[1] // NC

    cols = jnp.transpose(cache_values.reshape(ROWS // HD, HD, HD), (0, 2, 1)).reshape(ROWS, HD)
    b000 = jnp.concatenate([cache_keys, cols], axis=0)
    b300 = hop(b000, dz=1)
    b100 = hop(b000, dz=-1)
    b010 = hop(b000, dx=1)

    part = lax.dynamic_slice_in_dim(tokens, parity * few, few, 0)
    mine = trade(
        jnp.transpose(part.reshape(few, CHIPS, NC * depth), (1, 0, 2)), 0
    ).reshape(CHIPS * few, NC * depth)

    near = jnp.arange(few, dtype=jnp.int32)[None, None, :]
    kinds = jnp.stack([core, 1 - core])[:, None, None]
    of_chip = jnp.arange(CHIPS, dtype=jnp.int32)[None, :, None]
    index = (of_chip * 4 * few + kinds * 2 * few + near).reshape(-1) + span_start[0]
    turn_a = tables(index + parity * few)
    turn_b = tables(index + (1 - parity) * few)
    turn_kv = tables(
        span_start[0] + chip * 4 * few + jnp.arange(4 * few, dtype=jnp.int32)
    )

    q_got = hop(lax.dynamic_slice_in_dim(q_weight, (1 - core) * width, width, 1), dc=1)
    kv_got = hop(jnp.where(core == 0, v_weight, k_weight), dc=1)
    got = (q_got, kv_got)

    mine, got, b300, b100, b010, turn_a, turn_b, turn_kv = barrier(
        (mine, got, b300, b100, b010, turn_a, turn_b, turn_kv)
    )
    far = CHIPS * few // 2
    other = [hop_y(mine[:far], 1), hop_y(mine[far:], -1)]
    mine_twin = hop(mine, dc=1)

    def sums(parts):
        return project(core, parts, q_weight, k_weight, v_weight, got).astype(jnp.float16)

    half = SPAN // 2

    def total_of(parts):
        return jnp.sum(parts[:, :half].astype(jnp.float32), axis=0) * (1.0 / BOOST)

    def kv_of(parts):
        rows = jnp.sum(parts[:, half:].astype(jnp.float32), axis=0).reshape(2, NC, few, HD)
        return (rows[0] + rows[1] * (1.0 / LOW)) * (1.0 / BOOST)

    b310 = hop(b010, dz=1)
    b200 = hop(b100, dz=-1)
    b110 = hop(b100, dx=1)
    first_own = [b000, b300, b100, b010]

    sent_a = trade(sums([mine, mine_twin]), 0)
    other, b310, b200, b110 = barrier((other, b310, b200, b110))
    other_twin = [hop(x, dc=1) for x in other]
    first_swap = [hop(b, dc=1) for b in first_own]
    q_b = sums(other + other_twin)
    b210k = hop(b200[:ROWS], dx=1)
    b210v = hop(b310[ROWS:], dz=1)
    q_b, first_swap, b210k, b210v = barrier((q_b, first_swap, b210k, b210v))
    sent_b = trade(q_b, 0)
    second_own = [b310, b200, b110]
    second_swap = [hop(b, dc=1) for b in second_own]

    z_me, x_me = chip // NX, chip % NX
    pieces, places, slots = [], [], []

    def add(own, swap, dz, dx, first=0, fresh=True):
        if fresh:
            place = ((z_me + dz) % NZ) * NX * NC + ((x_me + dx) % NX) * NC
            slots.extend([place + core, place + 1 - core])
        pieces.extend([own, swap])
        places.extend([(len(slots) - 2, first), (len(slots) - 1, first)])

    for own, swap, (dz, dx) in zip(
        first_own + second_own,
        first_swap + second_swap,
        [(0, 0), (3, 0), (1, 0), (0, 1), (3, 1), (2, 0), (1, 1)],
    ):
        add(own, swap, dz, dx)
    add(b210k, hop(b210k, dc=1), 2, 1)
    add(b210v, hop(b210v, dc=1), 2, 1, ROWS, False)
    places = tuple(places)
    meta = jnp.stack([cache_len[0], core, parity] + slots).astype(jnp.int32)

    def attend(sent, turn):
        return attention_call(
            first_kernel,
            meta,
            [total_of(sent), *turn],
            pieces,
            places,
            (
                jax.ShapeDtypeStruct((HD, half), jnp.float32),
                jax.ShapeDtypeStruct((8, half), jnp.float32),
                jax.ShapeDtypeStruct((half, HD), jnp.bfloat16),
            ),
        )

    state_a = attend(sent_a, turn_a)
    sent_b, state_a = barrier((sent_b, state_a))
    state_b = attend(sent_b, turn_b)

    settled = settle(core, parity, kv_of(sent_a), kv_of(sent_b), *turn_kv)
    new = lax.all_to_all(settled, "ulysses", split_axis=0, concat_axis=0, tiled=True)
    new, state_b = barrier((new, state_b))
    mixed = attention_call(
        last_kernel,
        meta,
        [*state_a, *state_b, new],
        pieces,
        places,
        jax.ShapeDtypeStruct((CHIPS, NC, 2, few, HD), jnp.bfloat16),
    )
    n_all = n_tensor * NC * CHIPS
    out_rows = SPAN // n_all
    moved = lax.all_to_all(
        mixed.reshape(n_all, out_rows, HD),
        ("tensor", "ulysses"),
        split_axis=0,
        concat_axis=0,
        tiled=True,
    )
    moved = moved.reshape(n_tensor, CHIPS, NC, out_rows, HD)
    return jnp.transpose(moved, (3, 0, 2, 1, 4)).reshape(out_rows, n_all * HD)


def solution(mesh):
    placed = (
        P("ulysses", None),
        P("ulysses", "tensor"),
        P("ulysses", "tensor"),
        P("ulysses", "tensor"),
        P("ulysses", "tensor"),
        P("ulysses", "tensor"),
        P(),
        P(),
    )
    return jax.shard_map(
        on_device,
        mesh=mesh,
        in_specs=placed,
        out_specs=P(("tensor", "ulysses"), None),
        check_vma=False,
    )
```

time: 524 us -> 232 us (0.44)
  waiting for transfers between devices: 364 us -> 13.1 us
  Pallas kernels: 0 us -> 112 us
  matrix products: 75.9 us -> 0 us
  starting transfers between devices: 9.45 us -> 48.1 us
  other arithmetic: 30.4 us -> 16.8 us
  between operations: 13.9 us -> 1.59 us
  local copies, waits for them, and re-layouts: 11 us -> 18.3 us
  blocking collectives: 16.6 us -> 22 us
    psum x1 -> x0, waiting for transfers between devices: 125 us -> none  [on_device(): lax.psum(kv_part.astype(jnp.bfloat16), 'ulysses').astype(jnp.float32)]
    pallas_call x0 -> x6, Pallas kernels: none -> 112 us  [the longest x3 98.4 us: attention_call(): pl.pallas_call(functools.partial(kernel, places), in_specs=[pl.BlockSpec(...]
    all_gather x2 -> x0, waiting for transfers between devices: 110 us -> none  [the longest x1 55.9 us: on_device(): values_piece = lax.all_gather(cache_values, 'ulysses', axis=0, tiled=True)]
    reduce_scatter x1 -> x0, waiting for transfers between devices: 105 us -> none  [on_device(): lax.psum_scatter(jnp.transpose(term, (1, 0, 2, 3)).reshape(q_cols // n_ul...]
    dot_general x36 -> x0, matrix products: 75.9 us -> none  [the longest x16 36.6 us: one_block(): jnp.einsum('jgd,hgjc->hgdc', value_block, block_weights.astype(jnp.bfloat...]
    ppermute x0 -> x24, starting transfers between devices: none -> 25.8 us  [the longest x22 23.1 us: hop(): return lax.ppermute(values, 'ulysses', pairs)]
    all_to_all x1 -> x4, waiting for transfers between devices: 22.8 us -> 9.55 us  [the longest x3 9.55 us: trade(): lax.all_to_all(values, 'ulysses', split_axis=axis, concat_axis=axis, axis...]
    all_to_all x1 -> x4, starting transfers between devices: 9.29 us -> 22.3 us  [the longest x3 12.8 us: trade(): lax.all_to_all(values, 'ulysses', split_axis=axis, concat_axis=axis, axis...]
  transfers between devices with their start and end apart: 5 -> 28, of which waited for: 5 -> 5; matrix products, arithmetic and copies ran while one was open for 4% -> 9% of each run, Pallas kernels for 0% -> 14%
where the time goes in v2:
time: 232 us; the launch traced here: 231 us
  Pallas kernels  112 us (48%)
  starting transfers between devices  48.1 us (21%)
  blocking collectives  22 us (9%)
  local copies, waits for them, and re-layouts  18.3 us (8%)
  other arithmetic  16.8 us (7%)
  waiting for transfers between devices  13.1 us (6%)
    pallas_call x3, Pallas kernels, attention_call(): pl.pallas_call(functools.partial(kernel, places), in_specs=[pl.BlockSpec(...  98.4 us
    ppermute x22, starting transfers between devices, hop(): return lax.ppermute(values, 'ulysses', pairs)  23.1 us
    all_to_all x1, blocking collectives, on_device(): lax.all_to_all(mixed.reshape(n_all, out_rows, HD), ('tensor', 'ulysses'),...  22 us
    all_to_all x3, starting transfers between devices, trade(): lax.all_to_all(values, 'ulysses', split_axis=axis, concat_axis=axis, axis...  12.8 us
    pallas_call x2, Pallas kernels, project(): pl.pallas_call(functools.partial(project_kernel, len(parts)), grid_spec=p...  11.3 us
    all_to_all x3, waiting for transfers between devices, trade(): lax.all_to_all(values, 'ulysses', split_axis=axis, concat_axis=axis, axis...  9.55 us
    all_to_all x1, starting transfers between devices, on_device(): lax.all_to_all(settled, 'ulysses', split_axis=0, concat_axis=0, tiled=True)  9.49 us
    unnamed x29, local copies, waits for them, and re-layouts  7.75 us
  transfers between devices with their start and end apart: 28, of which 5 were waited for; matrix products, arithmetic and copies ran while one was open for 9% of the time, Pallas kernels for 14%

profile of v2, /device:TPU:1, one launch (start us, length us, event | category | flops | bytes accessed | tf_op | source)
XLA Modules:
  0.0 231.4 jit_solution(7879373574924426777)
XLA Ops:
  0.0 1.3 copy.15
  1.3 1.8 pad_maximum_fusion.rest_0_
  3.0 2.5 %collective-permute-start.2 = (bf16[2048,128]{1,0:T(8,128)(2,1)}, bf16[2048,128]{1,0:T(8,128)(2,1)}, u32[]{:S(2)}, u32[]{:S(2)}) collective-permute-start(bf16[2048,128]{1,0:T(8,128)(2,1)} %pad_maximum_fusion.rest_0_), channel_id=1, source_target_pairs={{0,4},{1,5},{2,6},{3,7},{4,8},{5,9},{6,10},{7,11},{8,12},{9,13},{1... | collective-permute-start | bytes 1572872 | tf_op jit(solution)/shard_map/ppermute | solution.py:48
  5.5 2.1 collective-permute-start.3
  7.6 2.7 %collective-permute-start.4 = (bf16[2048,128]{1,0:T(8,128)(2,1)}, bf16[2048,128]{1,0:T(8,128)(2,1)}, u32[]{:S(2)}, u32[]{:S(2)}) collective-permute-start(bf16[2048,128]{1,0:T(8,128)(2,1)} %pad_maximum_fusion.rest_0_), channel_id=1, source_target_pairs={{0,2},{1,3},{2,0},{3,1},{4,6},{5,7},{6,4},{7,5},{8,10},{9,11},{10,... | collective-permute-start | bytes 1572872 | tf_op jit(solution)/shard_map/ppermute | solution.py:48
  10.4 3.1 %constant_dynamic-slice_fusion = bf16[1024,1024]{1,0:T(8,128)(2,1)} fusion(bf16[1024,2048]{1,0:T(8,128)(2,1)} %rest_2_.1, s32[]{:T(128)S(6)} %select_n.92), kind=kLoop, calls=%fused_computation.38 | loop fusion | bytes 4194308 | tf_op jit(solution)/shard_map/dynamic_slice | solution.py:415
  13.5 1.2 collective-permute-start
  15.4 1.6 copy.14
  17.0 3.6 %all-to-all-start = ((bf16[8,32,2048]{2,1,0:T(8,128)(2,1)}), bf16[8,32,2048]{2,1,0:T(8,128)(2,1)S(1)}, u32[]{:S(2)}, u32[]{:S(2)}) async-start(bf16[8,32,2048]{2,1,0:T(8,128)(2,1)} %copy.14), calls=%async_computation | async-start | bytes 2097152 | tf_op jit(solution)/shard_map/all_to_all | solution.py:371
  23.3 1.9 fusion.1
  28.3 9.5 %all-to-all-done = bf16[8,32,2048]{2,1,0:T(8,128)(2,1)S(1)} async-done(((bf16[8,32,2048]{2,1,0:T(8,128)(2,1)}), bf16[8,32,2048]{2,1,0:T(8,128)(2,1)S(1)}, u32[]{:S(2)}, u32[]{:S(2)}) %all-to-all-start) | async-done | bytes 1048608 | tf_op jit(solution)/shard_map/all_to_all | solution.py:371
  39.8 1.3 collective-permute-start.5
  42.4 1.4 collective-permute-start.6
  44.5 2.2 copy-done.1
  46.7 5.5 %shard_map.83 = f32[8,640,128]{2,1,0:T(8,128)S(1)} custom-call(s32[1]{0:T(128)} %bitcast.meta, bf16[256,2048]{1,0:T(8,128)(2,1)S(1)} %bitcast.40, bf16[256,2048]{1,0:T(8,128)(2,1)S(1)} %collective-permute-done.18.rest_1_, bf16[1024,2048]{1,0:T(8,128)(2,1)S(1)} %copy-done.1, bf16[1024,1024]{1,0:T(8,128)(2,1)} %collective-permute-done.rest_5_.rest_3_, ...), custom_call_target="tpu_custom_call" | custom-call | flops 2147483648 | bytes 8388608 | tf_op jit(solution)/shard_map/pallas_call | solution.py:310
  52.1 1.2 convert_element_type.65
  53.4 5.5 %all-to-all-start.2 = ((f16[8,640,128]{2,1,0:T(8,128)(2,1)}), f16[8,640,128]{2,1,0:T(8,128)(2,1)}, u32[]{:S(2)}, u32[]{:S(2)}) async-start(f16[8,640,128]{2,1,0:T(8,128)(2,1)} %convert_element_type.65), calls=%async_computation.2 | async-start | bytes 2621440 | tf_op jit(solution)/shard_map/all_to_all | solution.py:371
  58.9 1.7 collective-permute-start.12
  65.5 3.4 %collective-permute-start.16 = (bf16[1024,128]{1,0:T(8,128)(2,1)S(1)}, bf16[1024,128]{1,0:T(8,128)(2,1)S(1)}, u32[]{:S(2)}, u32[]{:S(2)}) collective-permute-start(bf16[1024,128]{1,0:T(8,128)(2,1)S(1)} %slice.42), channel_id=1, source_target_pairs={{0,2},{1,3},{2,0},{3,1},{4,6},{5,7},{6,4},{7,5},{8,10},{9,11},{10,... | collective-permute-start | bytes 786440 | tf_op jit(solution)/shard_map/ppermute | solution.py:48
  70.1 2.2 copy-done.2
  72.3 5.8 %shard_map.82 = f32[8,640,128]{2,1,0:T(8,128)S(1)} custom-call(s32[1]{0:T(128)} %bitcast.meta, bf16[128,2048]{1,0:T(8,128)(2,1)} %collective-permute-done.5.rest_0_, bf16[128,2048]{1,0:T(8,128)(2,1)} %collective-permute-done.6.rest_1_, bf16[128,2048]{1,0:T(8,128)(2,1)S(1)} %collective-permute-done.10.rest_2_, ...), custom_call_target="tpu_custom_call" | custom-call | flops 2147483648 | bytes 8388608 | tf_op jit(solution)/shard_map/pallas_call | solution.py:310
  78.1 1.3 convert_element_type.64
  79.4 1.5 collective-permute-done.16.rest_14_
  82.7 3.7 %all-to-all-start.1 = ((f16[8,640,128]{2,1,0:T(8,128)(2,1)}), f16[8,640,128]{2,1,0:T(8,128)(2,1)S(1)}, u32[]{:S(2)}, u32[]{:S(2)}) async-start(f16[8,640,128]{2,1,0:T(8,128)(2,1)} %convert_element_type.64), calls=%async_computation.1 | async-start | bytes 2621440 | tf_op jit(solution)/shard_map/all_to_all | solution.py:371
  87.7 1.9 collective-permute-start.19
  91.3 1.4 convert_reduce_fusion.1
  94.2 11.1 %shard_map.84 = (f32[128,512]{1,0:T(8,128)}, f32[8,512]{1,0:T(8,128)}, bf16[512,128]{1,0:T(8,128)(2,1)}) custom-call(s32[19]{0:T(128)} %stack.87.meta, f32[512,128]{1,0:T(8,128)} %broadcast_multiply_fusion.1.q_ref, f32[512,128]{1,0:T(8,128)} %get-tuple-element.54.cos_ref, f32[512,128]{1,0:T(8,128)} %get-tuple-element.55.sin_ref, ...), custom_call_target="tpu_custom_call" | custom-call | flops 4563402752 | bytes 8388608 | tf_op jit(solution)/shard_map/pallas_call | solution.py:246
  108.5 1.9 shard_map.85
  110.3 9.5 %all-to-all-start.3 = ((bf16[16,128,128]{2,1,0:T(8,128)(2,1)}), bf16[16,128,128]{2,1,0:T(8,128)(2,1)S(1)}, u32[]{:S(2)}, u32[]{:S(2)}) async-start(bf16[16,128,128]{2,1,0:T(8,128)(2,1)} %shard_map.85), calls=%async_computation.3 | async-start | bytes 1048576 | tf_op jit(solution)/shard_map/all_to_all | solution.py:495
  120.6 11.1 %shard_map.86 = (f32[128,512]{1,0:T(8,128)}, f32[8,512]{1,0:T(8,128)}, bf16[512,128]{1,0:T(8,128)(2,1)}) custom-call(s32[19]{0:T(128)} %stack.87.meta, f32[512,128]{1,0:T(8,128)} %broadcast_multiply_fusion.q_ref, f32[512,128]{1,0:T(8,128)} %get-tuple-element.72.cos_ref, f32[512,128]{1,0:T(8,128)} %get-tuple-element.73.sin_ref, ...), custom_call_target="tpu_custom_call" | custom-call | flops 4563402752 | bytes 8388608 | tf_op jit(solution)/shard_map/pallas_call | solution.py:246
  132.4 76.2 %shard_map.87 = bf16[8,2,2,32,128]{4,3,2,1,0:T(8,128)(2,1)} custom-call(s32[19]{0:T(128)} %stack.87.meta, f32[128,512]{1,0:T(8,128)} %get-tuple-element.66.acc_a, f32[8,512]{1,0:T(8,128)} %get-tuple-element.67.total_a, bf16[512,128]{1,0:T(8,128)(2,1)} %get-tuple-element.68.turned_a, f32[128,512]{1,0:T(8,128)} %get-tuple-element.77.acc_b, ...), custom_call_target="tpu_custom_call" | custom-call | flops 4563402752 | bytes 8388608 | tf_op jit(solution)/shard_map/pallas_call | solution.py:246
  208.6 22.0 %all_to_all.25 = bf16[128,8,128]{2,1,0:T(8,128)(2,1)S(1)} all-to-all(bf16[128,8,128]{2,1,0:T(8,128)(2,1)} %bitcast.46), channel_id=1, replica_groups=mesh['tensor'=8,'ulysses'=16] {'tensor','ulysses'}, dimensions={0} | all-to-all | bytes 524288 | tf_op jit(solution)/shard_map/all_to_all | solution.py:507
  (95 shorter events, 26.7 us)
Async XLA Ops:
  0.0 14.7 %copy-start = (bf16[64,16384]{1,0:T(8,128)(2,1)S(1)}, bf16[64,16384]{1,0:T(8,128)(2,1)}, u32[]{:S(2)}) copy-start(bf16[64,16384]{1,0:T(8,128)(2,1)} %param.8) | copy-start | bytes 6291460
  3.0 25.2 %collective-permute-start.2 = (bf16[2048,128]{1,0:T(8,128)(2,1)}, bf16[2048,128]{1,0:T(8,128)(2,1)}, u32[]{:S(2)}, u32[]{:S(2)}) collective-permute-start(bf16[2048,128]{1,0:T(8,128)(2,1)} %pad_maximum_fusion.rest_0_), channel_id=1, source_target_pairs={{0,4},{1,5},{2,6},{3,7},{4,8},{5,9},{6,10},{7,11},{8,12},{9,13},{1... | collective-permute-start | bytes 1572872 | tf_op jit(solution)/shard_map/ppermute | solution.py:48
  5.5 22.8 %collective-permute-start.3 = (bf16[2048,128]{1,0:T(8,128)(2,1)}, bf16[2048,128]{1,0:T(8,128)(2,1)}, u32[]{:S(2)}, u32[]{:S(2)}) collective-permute-start(bf16[2048,128]{1,0:T(8,128)(2,1)} %pad_maximum_fusion.rest_0_), channel_id=1, source_target_pairs={{0,12},{1,13},{2,14},{3,15},{4,0},{5,1},{6,2},{7,3},{8,4},{9,5},{1... | collective-permute-start | bytes 1572872 | tf_op jit(solution)/shard_map/ppermute | solution.py:48
  7.6 20.6 %collective-permute-start.4 = (bf16[2048,128]{1,0:T(8,128)(2,1)}, bf16[2048,128]{1,0:T(8,128)(2,1)}, u32[]{:S(2)}, u32[]{:S(2)}) collective-permute-start(bf16[2048,128]{1,0:T(8,128)(2,1)} %pad_maximum_fusion.rest_0_), channel_id=1, source_target_pairs={{0,2},{1,3},{2,0},{3,1},{4,6},{5,7},{6,4},{7,5},{8,10},{9,11},{10,... | collective-permute-start | bytes 1572872 | tf_op jit(solution)/shard_map/ppermute | solution.py:48
  13.5 24.4 %collective-permute-start = (bf16[1024,1024]{1,0:T(8,128)(2,1)}, bf16[1024,1024]{1,0:T(8,128)(2,1)}, u32[]{:S(2)}, u32[]{:S(2)}) collective-permute-start(bf16[1024,1024]{1,0:T(8,128)(2,1)} %constant_dynamic-slice_fusion), channel_id=1, source_target_pairs={{0,1},{1,0},{2,3},{3,2},{4,5},{5,4},{6,7},{7,6},{8,9},{9,8},{10,11... | collective-permute-start | bytes 6291464 | tf_op jit(solution)/shard_map/ppermute | solution.py:48
  17.0 20.9 %all-to-all-start = ((bf16[8,32,2048]{2,1,0:T(8,128)(2,1)}), bf16[8,32,2048]{2,1,0:T(8,128)(2,1)S(1)}, u32[]{:S(2)}, u32[]{:S(2)}) async-start(bf16[8,32,2048]{2,1,0:T(8,128)(2,1)} %copy.14), calls=%async_computation | async-start | bytes 2097152 | tf_op jit(solution)/shard_map/all_to_all | solution.py:371
  21.3 7.0 %collective-permute-start.1 = (bf16[1024,128]{1,0:T(8,128)(2,1)}, bf16[1024,128]{1,0:T(8,128)(2,1)}, u32[]{:S(2)}, u32[]{:S(2)}) collective-permute-start(bf16[1024,128]{1,0:T(8,128)(2,1)} %broadcast_select_fusion), channel_id=1, source_target_pairs={{0,1},{1,0},{2,3},{3,2},{4,5},{5,4},{6,7},{7,6},{8,9},{9,8},{10,11... | collective-permute-start | bytes 786440 | tf_op jit(solution)/shard_map/ppermute | solution.py:48
  37.8 6.6 %copy-start.4 = (bf16[1024,128]{1,0:T(8,128)(2,1)S(1)}, bf16[1024,128]{1,0:T(8,128)(2,1)}, u32[]{:S(2)}) copy-start(bf16[1024,128]{1,0:T(8,128)(2,1)} %rest_5_.1) | copy-start | bytes 786436
  37.8 6.0 %collective-permute-start.18 = (bf16[256,2048]{1,0:T(8,128)(2,1)S(1)}, bf16[256,2048]{1,0:T(8,128)(2,1)S(1)}, u32[]{:S(2)}, u32[]{:S(2)}) collective-permute-start(bf16[256,2048]{1,0:T(8,128)(2,1)S(1)} %bitcast.38), channel_id=1, source_target_pairs={{0,1},{1,0},{2,3},{3,2},{4,5},{5,4},{6,7},{7,6},{8,9},{9,8},{10,11... | collective-permute-start | bytes 3145736 | tf_op jit(solution)/shard_map/ppermute | solution.py:48
  39.8 19.1 %collective-permute-start.5 = (bf16[128,2048]{1,0:T(8,128)(2,1)}, bf16[128,2048]{1,0:T(8,128)(2,1)}, u32[]{:S(2)}, u32[]{:S(2)}) collective-permute-start(bf16[128,2048]{1,0:T(8,128)(2,1)} %get-tuple-element.82), channel_id=1, source_target_pairs={{0,16},{16,32},{32,48},{48,0},{64,80},{80,96},{96,112},{112,64},{1... | collective-permute-start | bytes 1572872 | tf_op jit(solution)/shard_map/ppermute | solution.py:53
  41.1 19.6 %collective-permute-start.8 = (bf16[2048,128]{1,0:T(8,128)(2,1)}, bf16[2048,128]{1,0:T(8,128)(2,1)}, u32[]{:S(2)}, u32[]{:S(2)}) collective-permute-start(bf16[2048,128]{1,0:T(8,128)(2,1)} %collective-permute-done.3.rest_4_), channel_id=1, source_target_pairs={{0,12},{1,13},{2,14},{3,15},{4,0},{5,1},{6,2},{7,3},{8,4},{9,5},{1... | collective-permute-start | bytes 1572872 | tf_op jit(solution)/shard_map/ppermute | solution.py:48
  41.8 18.8 %collective-permute-start.9 = (bf16[2048,128]{1,0:T(8,128)(2,1)}, bf16[2048,128]{1,0:T(8,128)(2,1)}, u32[]{:S(2)}, u32[]{:S(2)}) collective-permute-start(bf16[2048,128]{1,0:T(8,128)(2,1)} %collective-permute-done.3.rest_4_), channel_id=1, source_target_pairs={{0,2},{1,3},{2,0},{3,1},{4,6},{5,7},{6,4},{7,5},{8,10},{9,11},{10,... | collective-permute-start | bytes 1572872 | tf_op jit(solution)/shard_map/ppermute | solution.py:48
  42.4 18.2 %collective-permute-start.6 = (bf16[128,2048]{1,0:T(8,128)(2,1)}, bf16[128,2048]{1,0:T(8,128)(2,1)}, u32[]{:S(2)}, u32[]{:S(2)}) collective-permute-start(bf16[128,2048]{1,0:T(8,128)(2,1)} %get-tuple-element.81), channel_id=1, source_target_pairs={{0,48},{16,0},{32,16},{48,32},{64,112},{80,64},{96,80},{112,96},{1... | collective-permute-start | bytes 1572872 | tf_op jit(solution)/shard_map/ppermute | solution.py:53
  43.9 16.7 %collective-permute-start.7 = (bf16[2048,128]{1,0:T(8,128)(2,1)}, bf16[2048,128]{1,0:T(8,128)(2,1)}, u32[]{:S(2)}, u32[]{:S(2)}) collective-permute-start(bf16[2048,128]{1,0:T(8,128)(2,1)} %collective-permute-done.4.rest_6_), channel_id=1, source_target_pairs={{0,4},{1,5},{2,6},{3,7},{4,8},{5,9},{6,10},{7,11},{8,12},{9,13},{1... | collective-permute-start | bytes 1572872 | tf_op jit(solution)/shard_map/ppermute | solution.py:48
  53.4 16.7 %copy-start.5 = (bf16[1024,128]{1,0:T(8,128)(2,1)S(1)}, bf16[1024,128]{1,0:T(8,128)(2,1)}, u32[]{:S(2)}) copy-start(bf16[1024,128]{1,0:T(8,128)(2,1)} %rest_5_.1) | copy-start | bytes 786436
  53.4 29.3 %all-to-all-start.2 = ((f16[8,640,128]{2,1,0:T(8,128)(2,1)}), f16[8,640,128]{2,1,0:T(8,128)(2,1)}, u32[]{:S(2)}, u32[]{:S(2)}) async-start(f16[8,640,128]{2,1,0:T(8,128)(2,1)} %convert_element_type.65), calls=%async_computation.2 | async-start | bytes 2621440 | tf_op jit(solution)/shard_map/all_to_all | solution.py:371
  58.9 3.4 %collective-permute-start.12 = (bf16[2048,128]{1,0:T(8,128)(2,1)}, bf16[2048,128]{1,0:T(8,128)(2,1)S(1)}, u32[]{:S(2)}, u32[]{:S(2)}) collective-permute-start(bf16[2048,128]{1,0:T(8,128)(2,1)} %pad_maximum_fusion.rest_0_), channel_id=1, source_target_pairs={{0,1},{1,0},{2,3},{3,2},{4,5},{5,4},{6,7},{7,6},{8,9},{9,8},{10,11... | collective-permute-start | bytes 1572872 | tf_op jit(solution)/shard_map/ppermute | solution.py:48
  60.6 4.9 %collective-permute-start.10 = (bf16[128,2048]{1,0:T(8,128)(2,1)}, bf16[128,2048]{1,0:T(8,128)(2,1)S(1)}, u32[]{:S(2)}, u32[]{:S(2)}) collective-permute-start(bf16[128,2048]{1,0:T(8,128)(2,1)} %collective-permute-done.5.rest_0_), channel_id=1, source_target_pairs={{0,1},{1,0},{2,3},{3,2},{4,5},{5,4},{6,7},{7,6},{8,9},{9,8},{10,11... | collective-permute-start | bytes 1572872 | tf_op jit(solution)/shard_map/ppermute | solution.py:48
  60.7 8.2 %collective-permute-start.11 = (bf16[128,2048]{1,0:T(8,128)(2,1)}, bf16[128,2048]{1,0:T(8,128)(2,1)S(1)}, u32[]{:S(2)}, u32[]{:S(2)}) collective-permute-start(bf16[128,2048]{1,0:T(8,128)(2,1)} %collective-permute-done.6.rest_1_), channel_id=1, source_target_pairs={{0,1},{1,0},{2,3},{3,2},{4,5},{5,4},{6,7},{7,6},{8,9},{9,8},{10,11... | collective-permute-start | bytes 1572872 | tf_op jit(solution)/shard_map/ppermute | solution.py:48
  61.2 18.2 %collective-permute-start.14 = (bf16[2048,128]{1,0:T(8,128)(2,1)}, bf16[2048,128]{1,0:T(8,128)(2,1)S(1)}, u32[]{:S(2)}, u32[]{:S(2)}) collective-permute-start(bf16[2048,128]{1,0:T(8,128)(2,1)} %collective-permute-done.3.rest_4_), channel_id=1, source_target_pairs={{0,1},{1,0},{2,3},{3,2},{4,5},{5,4},{6,7},{7,6},{8,9},{9,8},{10,11... | collective-permute-start | bytes 1572872 | tf_op jit(solution)/shard_map/ppermute | solution.py:48
  61.3 18.1 %collective-permute-start.13 = (bf16[2048,128]{1,0:T(8,128)(2,1)}, bf16[2048,128]{1,0:T(8,128)(2,1)S(1)}, u32[]{:S(2)}, u32[]{:S(2)}) collective-permute-start(bf16[2048,128]{1,0:T(8,128)(2,1)} %collective-permute-done.2.rest_2_), channel_id=1, source_target_pairs={{0,1},{1,0},{2,3},{3,2},{4,5},{5,4},{6,7},{7,6},{8,9},{9,8},{10,11... | collective-permute-start | bytes 1572872 | tf_op jit(solution)/shard_map/ppermute | solution.py:48
  63.2 16.2 %collective-permute-start.15 = (bf16[2048,128]{1,0:T(8,128)(2,1)}, bf16[2048,128]{1,0:T(8,128)(2,1)S(1)}, u32[]{:S(2)}, u32[]{:S(2)}) collective-permute-start(bf16[2048,128]{1,0:T(8,128)(2,1)} %collective-permute-done.4.rest_6_), channel_id=1, source_target_pairs={{0,1},{1,0},{2,3},{3,2},{4,5},{5,4},{6,7},{7,6},{8,9},{9,8},{10,11... | collective-permute-start | bytes 1572872 | tf_op jit(solution)/shard_map/ppermute | solution.py:48
  65.5 15.4 %collective-permute-start.16 = (bf16[1024,128]{1,0:T(8,128)(2,1)S(1)}, bf16[1024,128]{1,0:T(8,128)(2,1)S(1)}, u32[]{:S(2)}, u32[]{:S(2)}) collective-permute-start(bf16[1024,128]{1,0:T(8,128)(2,1)S(1)} %slice.42), channel_id=1, source_target_pairs={{0,2},{1,3},{2,0},{3,1},{4,6},{5,7},{6,4},{7,5},{8,10},{9,11},{10,... | collective-permute-start | bytes 786440 | tf_op jit(solution)/shard_map/ppermute | solution.py:48
  68.9 13.7 %collective-permute-start.17 = (bf16[1024,128]{1,0:T(8,128)(2,1)S(1)}, bf16[1024,128]{1,0:T(8,128)(2,1)}, u32[]{:S(2)}, u32[]{:S(2)}) collective-permute-start(bf16[1024,128]{1,0:T(8,128)(2,1)S(1)} %slice.43), channel_id=1, source_target_pairs={{0,4},{1,5},{2,6},{3,7},{4,8},{5,9},{6,10},{7,11},{8,12},{9,13},{1... | collective-permute-start | bytes 786440 | tf_op jit(solution)/shard_map/ppermute | solution.py:48
  82.7 22.7 %all-to-all-start.1 = ((f16[8,640,128]{2,1,0:T(8,128)(2,1)}), f16[8,640,128]{2,1,0:T(8,128)(2,1)S(1)}, u32[]{:S(2)}, u32[]{:S(2)}) async-start(f16[8,640,128]{2,1,0:T(8,128)(2,1)} %convert_element_type.64), calls=%async_computation.1 | async-start | bytes 2621440 | tf_op jit(solution)/shard_map/all_to_all | solution.py:371
  87.7 5.7 %collective-permute-start.19 = (bf16[2048,128]{1,0:T(8,128)(2,1)}, bf16[2048,128]{1,0:T(8,128)(2,1)S(1)}, u32[]{:S(2)}, u32[]{:S(2)}) collective-permute-start(bf16[2048,128]{1,0:T(8,128)(2,1)} %collective-permute-done.7.rest_8_), channel_id=1, source_target_pairs={{0,1},{1,0},{2,3},{3,2},{4,5},{5,4},{6,7},{7,6},{8,9},{9,8},{10,11... | collective-permute-start | bytes 1572872 | tf_op jit(solution)/shard_map/ppermute | solution.py:48
  89.6 3.8 %collective-permute-start.20 = (bf16[2048,128]{1,0:T(8,128)(2,1)}, bf16[2048,128]{1,0:T(8,128)(2,1)}, u32[]{:S(2)}, u32[]{:S(2)}) collective-permute-start(bf16[2048,128]{1,0:T(8,128)(2,1)} %collective-permute-done.8.rest_10_), channel_id=1, source_target_pairs={{0,1},{1,0},{2,3},{3,2},{4,5},{5,4},{6,7},{7,6},{8,9},{9,8},{10,11... | collective-permute-start | bytes 1572872 | tf_op jit(solution)/shard_map/ppermute | solution.py:48
  89.6 3.8 %collective-permute-start.21 = (bf16[2048,128]{1,0:T(8,128)(2,1)}, bf16[2048,128]{1,0:T(8,128)(2,1)}, u32[]{:S(2)}, u32[]{:S(2)}) collective-permute-start(bf16[2048,128]{1,0:T(8,128)(2,1)} %collective-permute-done.9.rest_12_), channel_id=1, source_target_pairs={{0,1},{1,0},{2,3},{3,2},{4,5},{5,4},{6,7},{7,6},{8,9},{9,8},{10,11... | collective-permute-start | bytes 1572872 | tf_op jit(solution)/shard_map/ppermute | solution.py:48
  90.8 2.6 %collective-permute-start.22 = (bf16[1024,128]{1,0:T(8,128)(2,1)}, bf16[1024,128]{1,0:T(8,128)(2,1)}, u32[]{:S(2)}, u32[]{:S(2)}) collective-permute-start(bf16[1024,128]{1,0:T(8,128)(2,1)} %copy-done.13), channel_id=1, source_target_pairs={{0,1},{1,0},{2,3},{3,2},{4,5},{5,4},{6,7},{7,6},{8,9},{9,8},{10,11... | collective-permute-start | bytes 786440 | tf_op jit(solution)/shard_map/ppermute | solution.py:48
  90.8 3.0 %collective-permute-start.23 = (bf16[1024,128]{1,0:T(8,128)(2,1)}, bf16[1024,128]{1,0:T(8,128)(2,1)}, u32[]{:S(2)}, u32[]{:S(2)}) collective-permute-start(bf16[1024,128]{1,0:T(8,128)(2,1)} %collective-permute-done.17.rest_16_), channel_id=1, source_target_pairs={{0,1},{1,0},{2,3},{3,2},{4,5},{5,4},{6,7},{7,6},{8,9},{9,8},{10,11... | collective-permute-start | bytes 786440 | tf_op jit(solution)/shard_map/ppermute | solution.py:48
  106.2 13.6 %copy-start.6 = (f32[512,128]{1,0:T(8,128)S(1)}, f32[512,128]{1,0:T(8,128)}, u32[]{:S(2)}) copy-start(f32[512,128]{1,0:T(8,128)} %convert_reduce_fusion) | copy-start | bytes 786436
  110.3 21.3 %all-to-all-start.3 = ((bf16[16,128,128]{2,1,0:T(8,128)(2,1)}), bf16[16,128,128]{2,1,0:T(8,128)(2,1)S(1)}, u32[]{:S(2)}, u32[]{:S(2)}) async-start(bf16[16,128,128]{2,1,0:T(8,128)(2,1)} %shard_map.85), calls=%async_computation.3 | async-start | bytes 1048576 | tf_op jit(solution)/shard_map/all_to_all | solution.py:495
  (10 other events, 17.2 us)
